TPU v7x, 512 devices: a whole 4x8x8 slice. The times are simulated.
512 devices in a mesh: slab: 16 (over z, y_hi), head: 8 (over y_lo, core), dp: 4 (over x).
Axes of the slice: x: 4, y: 8 (y_hi: 2, y_lo: 4; y = y_hi * 4 + y_lo), z: 8, core: 2. Of those that a mesh axis runs over, the one named last changes fastest.
Arguments:
- q_proj: bfloat16 [4, 6144, 2048], P('dp', ('slab', 'head')), may hold values from -6 to 6
- k_proj: bfloat16 [4, 6144, 2048], P('dp', ('slab', 'head')), may hold values from -6 to 6
- v_proj: bfloat16 [4, 6144, 2048], P('dp', ('slab', 'head')), may hold values from -6 to 6
- grad_out: bfloat16 [4, 6144, 2048], P('dp', ('slab', 'head')), may hold values from -6 to 6
- norm_gains: float32 [2, 128], replicated, may hold values from 0.5 to 1.5
- window_mask: int32 [4, 16, 3], P('dp'), may hold values from 0 to 1, as said below
Outputs:
- attended: bfloat16 [4, 6144, 2048], P('dp', ('slab', 'head'))
- q_grad: bfloat16 [4, 6144, 2048], P('dp', ('slab', 'head'))
- k_grad: bfloat16 [4, 6144, 2048], P('dp', ('slab', 'head'))
- v_grad: bfloat16 [4, 6144, 2048], P('dp', ('slab', 'head'))
- gain_grads: float32 [2, 128], replicated
Inputs may be any that keep to these rules, and one draw needn't show every extreme that they name: window_mask[c, t, j] is 0 or 1; the middle slot j = 1 is always 1, and slots that point before the first or after the last of the clip's 16 tiles are 0.
All inputs are finite; a program needn't handle non-finite values.
Results may differ from a plain program's by a relative error of at most 0.0095.
Values may be sent and summed in bfloat16 or wider, within the bound.
A program may use at most 64 MiB of HBM per device.

v0:
```python
import jax
import jax.numpy as jnp
from jax import lax
from jax.sharding import PartitionSpec as P

TILE = 384


EPS = 1e-06


def with_halo(shard, sides, width):
    for axis, dim in sides:
        devices, length = (lax.axis_size(axis), shard.shape[dim])
        up = [(i, (i + 1) % devices) for i in range(devices - 1)]
        down = [(j, i) for i, j in up]
        last = lax.slice_in_dim(shard, length - width, length, axis=dim)
        leading = lax.slice_in_dim(shard, 0, width, axis=dim)
        before = lax.ppermute(last, axis, up)
        after = lax.ppermute(leading, axis, down)
        shard = jnp.concatenate([before, shard, after], axis=dim)
    return shard


def passed_along(value, axis, steps):
    count = lax.axis_size(axis)
    leading, last = (max(0, -steps), min(count, count - steps))
    return lax.ppermute(value, axis, [(source, source + steps) for source in range(leading, last)])


def rms_norm(raw, gain):
    values = raw.astype(jnp.float32)
    inverse = lax.rsqrt(jnp.mean(values * values, axis=-1, keepdims=True) + EPS)
    unit = values * inverse
    return (unit, inverse, (unit * gain).astype(jnp.bfloat16))


def norm_backward(unit, inverse, gain, grad):
    inner = grad * gain
    return inverse * (inner - unit * jnp.mean(inner * unit, axis=-1, keepdims=True))


def local(q_proj, k_proj, v_proj, grad_out, norm_gains, window_mask):
    q_loc, k_loc, v_loc, d_loc = (
        lax.all_to_all(q_proj, "head", split_axis=2, concat_axis=1, tiled=True),
        lax.all_to_all(k_proj, "head", split_axis=2, concat_axis=1, tiled=True),
        lax.all_to_all(v_proj, "head", split_axis=2, concat_axis=1, tiled=True),
        lax.all_to_all(grad_out, "head", split_axis=2, concat_axis=1, tiled=True),
    )
    rows = q_loc.shape[1]
    width = q_loc.shape[2]
    head_dim = norm_gains.shape[1]
    heads_here = width // head_dim
    window = window_mask.shape[2]
    radius = window // 2
    margin = radius * TILE
    span = window * TILE
    tiles_here = rows // TILE
    scale = head_dim ** (-0.5)
    shape3 = (rows, heads_here, head_dim)
    q_unit, q_inv, q_norm = rms_norm(q_loc[0].reshape(shape3), norm_gains[0])
    k_unit, k_inv, k_norm = rms_norm(k_loc[0].reshape(shape3), norm_gains[1])
    dout = d_loc[0].reshape(shape3)
    masks = window_mask[0]
    first = lax.axis_index("slab") * tiles_here
    keyval = jnp.concatenate([k_norm.reshape(rows, width), v_loc[0]], axis=1)
    wide = with_halo(keyval, (("slab", 0),), margin)
    buffer = jnp.zeros((rows + 2 * margin, 2 * width), jnp.float32)
    keys = wide[0:span, :width].reshape(span, heads_here, head_dim)
    vals = wide[0:span, width:].reshape(span, heads_here, head_dim)
    row = lax.dynamic_slice_in_dim(masks, first + 0, 1, 0)[0]
    colf = jnp.repeat(row, TILE).astype(jnp.float32)
    score = jnp.einsum("qhd,khd->hqk", q_norm, keys, preferred_element_type=jnp.float32) * scale
    expo = jnp.exp(score) * colf[None, None, :]
    denom = jnp.sum(expo, axis=-1)
    prob = (expo / denom[..., None]).astype(jnp.bfloat16)
    out_tile = jnp.einsum("hqk,khd->qhd", prob, vals, preferred_element_type=jnp.float32).astype(
        jnp.bfloat16
    )
    delta = jnp.sum(dout.astype(jnp.float32) * out_tile.astype(jnp.float32), axis=-1)
    dprob = jnp.einsum("qhd,khd->hqk", dout, vals, preferred_element_type=jnp.float32)
    dscore = (prob.astype(jnp.float32) * (dprob - delta.T[..., None])).astype(jnp.bfloat16)
    dq_parts = jnp.einsum("hqk,khd->qhd", dscore, keys, preferred_element_type=jnp.float32) * scale
    hi_row = window * TILE
    dk_part = jnp.einsum("hqk,qhd->khd", dscore, q_norm, preferred_element_type=jnp.float32) * scale
    dv_part = jnp.einsum("hqk,qhd->khd", prob, dout, preferred_element_type=jnp.float32)
    joined = jnp.concatenate(
        [dk_part.reshape(hi_row, width), dv_part.reshape(hi_row, width)], axis=1
    )
    buffer = buffer.at[0:hi_row].add(joined)
    lower = buffer[:margin]
    upper = buffer[rows + margin :]
    middle = buffer[margin : rows + margin]
    from_above = passed_along(lower.astype(jnp.bfloat16), "slab", -1).astype(lower.dtype)
    from_below = passed_along(upper.astype(jnp.bfloat16), "slab", 1).astype(upper.dtype)
    middle = middle.at[:margin].add(from_below)
    middle = middle.at[rows - margin :].add(from_above)
    dk_norm = middle[:, :width].reshape(shape3)
    dv_full = middle[:, width:]
    q_grad = norm_backward(q_unit, q_inv, norm_gains[0], dq_parts).astype(jnp.bfloat16)
    k_grad = norm_backward(k_unit, k_inv, norm_gains[1], dk_norm).astype(jnp.bfloat16)
    v_grad = dv_full.astype(jnp.bfloat16)
    gain_part = jnp.stack(
        [jnp.sum(dq_parts * q_unit, axis=(0, 1)), jnp.sum(dk_norm * k_unit, axis=(0, 1))]
    )
    gain_total = lax.psum(gain_part, ("slab", "head", "dp"))
    count = lax.axis_size("dp") * lax.axis_size("slab") * rows * lax.axis_size("head") * heads_here
    gain_grads = gain_total / jnp.sqrt(jnp.float32(count))
    results = (
        lax.all_to_all(
            out_tile.reshape(1, rows, width), "head", split_axis=1, concat_axis=2, tiled=True
        ),
        lax.all_to_all(
            q_grad.reshape(1, rows, width), "head", split_axis=1, concat_axis=2, tiled=True
        ),
        lax.all_to_all(
            k_grad.reshape(1, rows, width), "head", split_axis=1, concat_axis=2, tiled=True
        ),
        lax.all_to_all(
            v_grad.reshape(1, rows, width), "head", split_axis=1, concat_axis=2, tiled=True
        ),
    )
    return (results[0], results[1], results[2], results[3], gain_grads)


def solution(mesh):
    placed = (
        P("dp", ("slab", "head"), None),
        P("dp", ("slab", "head"), None),
        P("dp", ("slab", "head"), None),
        P("dp", ("slab", "head"), None),
        P(),
        P("dp", None, None),
    )
    return jax.shard_map(
        local,
        mesh=mesh,
        in_specs=placed,
        out_specs=(
            P("dp", ("slab", "head"), None),
            P("dp", ("slab", "head"), None),
            P("dp", ("slab", "head"), None),
            P("dp", ("slab", "head"), None),
            P(),
        ),
        check_vma=False,
    )
```

profile of v0, /device:TPU:1, one launch (start us, length us, event | category | flops | bytes accessed | tf_op | source)
XLA Modules:
  0.0 346.0 jit_solution(112783254505454189)
XLA Ops:
  0.6 2.2 copy.208
  3.3 11.5 %reduce.14 = bf16[2048,48]{1,0:T(8,128)(2,1)S(1)} reduce(bf16[2048,1,48]{2,1,0:T(2,128)(2,1)S(1)} %bitcast.173, bf16[]{:T(256)} %broadcast.134), dimensions={1}, to_apply=%bitcast.131.reduce_sub_computation | reduce | bytes 393218
  14.9 1.4 reshape.210
  16.3 10.7 %all-to-all-start.1 = ((bf16[8,2,6144]{2,1,0:T(2,128)(2,1)}), bf16[8,2,6144]{2,1,0:T(2,128)(2,1)S(1)}, u32[]{:S(2)}, u32[]{:S(2)}) async-start(bf16[8,2,6144]{2,1,0:T(2,128)(2,1)} %reshape.210), calls=%async_computation.1 | async-start | bytes 393216 | tf_op jit(solution)/shard_map/all_to_all | solution.py:47
  27.1 0.7 copy.202
  27.8 11.5 %reduce.15 = bf16[2048,48]{1,0:T(8,128)(2,1)S(1)} reduce(bf16[2048,1,48]{2,1,0:T(2,128)(2,1)S(1)} %bitcast.174, bf16[]{:T(256)} %broadcast.134), dimensions={1}, to_apply=%bitcast.133.reduce_sub_computation | reduce | bytes 393218
  39.4 1.4 reshape.212
  41.9 5.3 %all-to-all-start = ((bf16[8,2,6144]{2,1,0:T(2,128)(2,1)}), bf16[8,2,6144]{2,1,0:T(2,128)(2,1)S(1)}, u32[]{:S(2)}, u32[]{:S(2)}) async-start(bf16[8,2,6144]{2,1,0:T(2,128)(2,1)} %reshape.212), calls=%async_computation | async-start | bytes 393216 | tf_op jit(solution)/shard_map/all_to_all | solution.py:46
  47.3 0.7 copy.221
  48.1 11.5 %reduce.13 = bf16[2048,48]{1,0:T(8,128)(2,1)S(1)} reduce(bf16[2048,1,48]{2,1,0:T(2,128)(2,1)S(1)} %bitcast.175, bf16[]{:T(256)} %broadcast.134), dimensions={1}, to_apply=%bitcast.139.reduce_sub_computation | reduce | bytes 393218
  59.6 1.4 reshape.218
  61.3 0.7 copy.212
  62.1 11.7 %reduce.16 = bf16[2048,48]{1,0:T(8,128)(2,1)S(1)} reduce(bf16[2048,1,48]{2,1,0:T(2,128)(2,1)S(1)} %bitcast.176, bf16[]{:T(256)} %broadcast.134), dimensions={1}, to_apply=%bitcast.135.reduce_sub_computation | reduce | bytes 393218
  73.8 1.4 reshape.214
  75.3 1.0 reshape.211
  77.0 5.1 %all-to-all-start.4 = ((bf16[8,2,6144]{2,1,0:T(2,128)(2,1)}), bf16[8,2,6144]{2,1,0:T(2,128)(2,1)S(1)}, u32[]{:S(2)}, u32[]{:S(2)}) async-start(bf16[8,2,6144]{2,1,0:T(2,128)(2,1)} %reshape.218), calls=%async_computation.4 | async-start | bytes 393216 | tf_op jit(solution)/shard_map/all_to_all | solution.py:48
  82.1 1.0 reshape.213
  84.7 3.9 %all-to-all-done.4 = bf16[8,2,6144]{2,1,0:T(2,128)(2,1)S(1)} async-done(((bf16[8,2,6144]{2,1,0:T(2,128)(2,1)}), bf16[8,2,6144]{2,1,0:T(2,128)(2,1)S(1)}, u32[]{:S(2)}, u32[]{:S(2)}) %all-to-all-start.4) | async-done | bytes 196640 | tf_op jit(solution)/shard_map/all_to_all | solution.py:48
  88.6 5.2 %all-to-all-start.2 = ((bf16[8,2,6144]{2,1,0:T(2,128)(2,1)}), bf16[8,2,6144]{2,1,0:T(2,128)(2,1)S(1)}, u32[]{:S(2)}, u32[]{:S(2)}) async-start(bf16[8,2,6144]{2,1,0:T(2,128)(2,1)} %reshape.214), calls=%async_computation.2 | async-start | bytes 393216 | tf_op jit(solution)/shard_map/all_to_all | solution.py:45
  94.3 0.8 pad_maximum_fusion.2
  95.0 1.3 collective-permute-start.1
  96.3 8.7 %collective-permute-start = (bf16[384,512]{1,0:T(8,128)(2,1)}, bf16[384,512]{1,0:T(8,128)(2,1)}, u32[]{:S(2)}, u32[]{:S(2)}) collective-permute-start(bf16[384,512]{1,0:T(8,128)(2,1)} %pad_maximum_fusion.2), channel_id=1, source_target_pairs={{0,32},{32,64},{64,96},{96,128},{128,160},{160,192},{192,224},{224... | collective-permute-start | bytes 1179656 | tf_op jit(solution)/shard_map/ppermute | solution.py:19
  105.0 1.0 reshape.219
  106.6 0.7 copy.254
  107.3 1.0 reshape.215
  108.4 1.1 bitcast_convert_fusion
  109.6 0.8 copy.226
  111.9 0.8 collective-permute-done
  112.7 1.2 pad_maximum_fusion.1
  114.3 1.1 copy.216
  115.4 2.2 divide_convert_fusion
  117.7 2.5 fusion.23
  120.2 1.3 multiply_reduce_fusion.2
  121.5 1.9 copy.219
  123.5 3.4 reduce.17
  126.9 1.7 reshape.216
  128.5 19.2 %all-to-all-start.3 = ((bf16[8,2,6144]{2,1,0:T(2,128)(2,1)}), bf16[8,2,6144]{2,1,0:T(2,128)(2,1)}, u32[]{:S(2)}, u32[]{:S(2)}) async-start(bf16[8,2,6144]{2,1,0:T(2,128)(2,1)} %reshape.216), calls=%async_computation.3 | async-start | bytes 393216 | tf_op jit(solution)/shard_map/all_to_all | solution.py:110
  147.7 1.6 fusion.4
  150.4 2.0 fusion.13
  152.7 1.6 copy.232
  154.5 0.9 fusion.21
  155.4 1.5 collective-permute-start.3
  157.0 12.2 %collective-permute-start.2 = (bf16[384,512]{1,0:T(8,128)(2,1)}, bf16[384,512]{1,0:T(8,128)(2,1)}, u32[]{:S(2)}, u32[]{:S(2)}) collective-permute-start(bf16[384,512]{1,0:T(8,128)(2,1)} %get-tuple-element.69), channel_id=1, source_target_pairs={{0,32},{32,64},{64,96},{96,128},{128,160},{160,192},{192,224},{224... | collective-permute-start | bytes 1179656 | tf_op jit(solution)/shard_map/ppermute | solution.py:28
  169.2 0.8 fusion.16
  170.0 1.4 copy.228
  171.4 2.5 reduce.18
  173.9 1.7 reshape.220
  176.1 1.9 collective-permute-done.2
  178.0 1.2 fusion.9
  179.3 0.9 copy-done
  180.4 0.7 copy-done.3
  181.1 1.8 multiply_reduce_fusion.1
  183.0 17.4 %all-to-all-start.5 = ((bf16[8,2,6144]{2,1,0:T(2,128)(2,1)}), bf16[8,2,6144]{2,1,0:T(2,128)(2,1)S(1)}, u32[]{:S(2)}, u32[]{:S(2)}) async-start(bf16[8,2,6144]{2,1,0:T(2,128)(2,1)} %reshape.220), calls=%async_computation.5 | async-start | bytes 393216 | tf_op jit(solution)/shard_map/all_to_all | solution.py:113
  201.4 1.8 reduce.19
  203.2 0.7 reshape.222
  203.9 3.0 all-to-all-done.5
  206.9 5.2 %all-to-all-start.6 = ((bf16[8,2,6144]{2,1,0:T(2,128)(2,1)}), bf16[8,2,6144]{2,1,0:T(2,128)(2,1)S(1)}, u32[]{:S(2)}, u32[]{:S(2)}) async-start(bf16[8,2,6144]{2,1,0:T(2,128)(2,1)} %reshape.222), calls=%async_computation.6 | async-start | bytes 393216 | tf_op jit(solution)/shard_map/all_to_all | solution.py:116
  212.0 1.6 reshape.217
  213.7 0.7 copy.247
  214.6 0.7 copy.248
  215.6 1.8 reduce.20
  217.4 0.7 reshape.224
  218.5 5.2 %all-to-all-start.7 = ((bf16[8,2,6144]{2,1,0:T(2,128)(2,1)}), bf16[8,2,6144]{2,1,0:T(2,128)(2,1)S(1)}, u32[]{:S(2)}, u32[]{:S(2)}) async-start(bf16[8,2,6144]{2,1,0:T(2,128)(2,1)} %reshape.224), calls=%async_computation.7 | async-start | bytes 393216 | tf_op jit(solution)/shard_map/all_to_all | solution.py:119
  223.7 119.5 %psum.7 = f32[2,128]{1,0:T(2,128)S(1)} all-reduce(f32[2,128]{1,0:T(2,128)S(1)} %pad_maximum_fusion.3), channel_id=1, replica_groups=mesh['slab'=16,'head'=8,'dp'=4] {'slab','head','dp'}, use_global_device_ids=true, to_apply=%region_9.0 | all-reduce | flops 256 | bytes 2048 | tf_op jit(solution)/shard_map/psum | solution.py:106
  (100 shorter events, 13.7 us)
Async XLA Ops:
  0.6 26.4 %copy-start.9 = (bf16[1,48,2048]{2,1,0:T(8,128)(2,1)S(1)}, bf16[1,48,2048]{2,1,0:T(8,128)(2,1)}, u32[]{:S(2)}) copy-start(bf16[1,48,2048]{2,1,0:T(8,128)(2,1)} %param.19) | copy-start | bytes 589828
  16.3 25.6 %all-to-all-start.1 = ((bf16[8,2,6144]{2,1,0:T(2,128)(2,1)}), bf16[8,2,6144]{2,1,0:T(2,128)(2,1)S(1)}, u32[]{:S(2)}, u32[]{:S(2)}) async-start(bf16[8,2,6144]{2,1,0:T(2,128)(2,1)} %reshape.210), calls=%async_computation.1 | async-start | bytes 393216 | tf_op jit(solution)/shard_map/all_to_all | solution.py:47
  27.1 13.8 %copy-start.18 = (f32[2,128]{1,0:T(2,128)S(1)}, f32[2,128]{1,0:T(2,128)}, u32[]{:S(2)}) copy-start(f32[2,128]{1,0:T(2,128)} %param.22) | copy-start | bytes 3076
  27.1 20.2 %copy-start.10 = (bf16[1,48,2048]{2,1,0:T(8,128)(2,1)S(1)}, bf16[1,48,2048]{2,1,0:T(8,128)(2,1)}, u32[]{:S(2)}) copy-start(bf16[1,48,2048]{2,1,0:T(8,128)(2,1)} %param.21) | copy-start | bytes 589828
  41.9 5.4 %copy-start.13 = (f32[128]{0:T(128)}, f32[128]{0:T(128)S(1)}, u32[]{:S(2)}) copy-start(f32[128]{0:T(128)S(1)} %get-tuple-element.74) | copy-start | bytes 1540
  41.9 35.1 %all-to-all-start = ((bf16[8,2,6144]{2,1,0:T(2,128)(2,1)}), bf16[8,2,6144]{2,1,0:T(2,128)(2,1)S(1)}, u32[]{:S(2)}, u32[]{:S(2)}) async-start(bf16[8,2,6144]{2,1,0:T(2,128)(2,1)} %reshape.212), calls=%async_computation | async-start | bytes 393216 | tf_op jit(solution)/shard_map/all_to_all | solution.py:46
  47.3 13.8 %copy-start.17 = (s32[1,16,3]{1,0,2:T(1,128)S(1)}, s32[1,16,3]{1,0,2:T(1,128)}, u32[]{:S(2)}) copy-start(s32[1,16,3]{1,0,2:T(1,128)} %param.23) | copy-start | bytes 580
  47.3 14.0 %copy-start.11 = (bf16[1,48,2048]{2,1,0:T(8,128)(2,1)S(1)}, bf16[1,48,2048]{2,1,0:T(8,128)(2,1)}, u32[]{:S(2)}) copy-start(bf16[1,48,2048]{2,1,0:T(8,128)(2,1)} %param.18) | copy-start | bytes 589828
  77.0 11.6 %all-to-all-start.4 = ((bf16[8,2,6144]{2,1,0:T(2,128)(2,1)}), bf16[8,2,6144]{2,1,0:T(2,128)(2,1)S(1)}, u32[]{:S(2)}, u32[]{:S(2)}) async-start(bf16[8,2,6144]{2,1,0:T(2,128)(2,1)} %reshape.218), calls=%async_computation.4 | async-start | bytes 393216 | tf_op jit(solution)/shard_map/all_to_all | solution.py:48
  84.1 10.9 %copy-start.2 = (f32[384,2,128]{2,1,0:T(2,128)}, f32[384,2,128]{2,1,0:T(2,128)S(1)}, u32[]{:S(2)}) copy-start(f32[384,2,128]{2,1,0:T(2,128)S(1)} %reshape.204) | copy-start | bytes 1179652
  84.7 11.7 %copy-start.6 = (f32[384,2]{1,0:T(8,128)}, f32[384,2]{1,0:T(8,128)S(1)}, u32[]{:S(2)}) copy-start(f32[384,2]{1,0:T(8,128)S(1)} %add_rsqrt_fusion) | copy-start | bytes 9220
  88.6 18.8 %all-to-all-start.2 = ((bf16[8,2,6144]{2,1,0:T(2,128)(2,1)}), bf16[8,2,6144]{2,1,0:T(2,128)(2,1)S(1)}, u32[]{:S(2)}, u32[]{:S(2)}) async-start(bf16[8,2,6144]{2,1,0:T(2,128)(2,1)} %reshape.214), calls=%async_computation.2 | async-start | bytes 393216 | tf_op jit(solution)/shard_map/all_to_all | solution.py:45
  95.0 16.9 %collective-permute-start.1 = (bf16[384,512]{1,0:T(8,128)(2,1)}, bf16[384,512]{1,0:T(8,128)(2,1)}, u32[]{:S(2)}, u32[]{:S(2)}) collective-permute-start(bf16[384,512]{1,0:T(8,128)(2,1)} %pad_maximum_fusion.2), channel_id=1, source_target_pairs={{32,0},{64,32},{96,64},{128,96},{160,128},{192,160},{224,192},{256... | collective-permute-start | bytes 1179656 | tf_op jit(solution)/shard_map/ppermute | solution.py:20
  96.3 16.4 %collective-permute-start = (bf16[384,512]{1,0:T(8,128)(2,1)}, bf16[384,512]{1,0:T(8,128)(2,1)}, u32[]{:S(2)}, u32[]{:S(2)}) collective-permute-start(bf16[384,512]{1,0:T(8,128)(2,1)} %pad_maximum_fusion.2), channel_id=1, source_target_pairs={{0,32},{32,64},{64,96},{96,128},{128,160},{160,192},{192,224},{224... | collective-permute-start | bytes 1179656 | tf_op jit(solution)/shard_map/ppermute | solution.py:19
  108.3 1.1 copy-start.8
  117.7 2.5 copy-start.4
  128.5 54.5 %all-to-all-start.3 = ((bf16[8,2,6144]{2,1,0:T(2,128)(2,1)}), bf16[8,2,6144]{2,1,0:T(2,128)(2,1)}, u32[]{:S(2)}, u32[]{:S(2)}) async-start(bf16[8,2,6144]{2,1,0:T(2,128)(2,1)} %reshape.216), calls=%async_computation.3 | async-start | bytes 393216 | tf_op jit(solution)/shard_map/all_to_all | solution.py:110
  147.7 1.6 copy-start.15
  149.3 1.1 copy-start.5
  149.3 1.1 copy-start.12
  154.4 14.8 %copy-start.7 = (f32[2,128,384]{2,1,0:T(8,128)S(1)}, f32[2,128,384]{2,1,0:T(8,128)}, u32[]{:S(2)}) copy-start(f32[2,128,384]{2,1,0:T(8,128)} %get-tuple-element.77) | copy-start | bytes 1179652
  155.4 20.7 %collective-permute-start.3 = (bf16[384,512]{1,0:T(8,128)(2,1)}, bf16[384,512]{1,0:T(8,128)(2,1)}, u32[]{:S(2)}, u32[]{:S(2)}) collective-permute-start(bf16[384,512]{1,0:T(8,128)(2,1)} %get-tuple-element.70), channel_id=1, source_target_pairs={{32,0},{64,32},{96,64},{128,96},{160,128},{192,160},{224,192},{256... | collective-permute-start | bytes 1179656 | tf_op jit(solution)/shard_map/ppermute | solution.py:28
  157.0 21.0 %collective-permute-start.2 = (bf16[384,512]{1,0:T(8,128)(2,1)}, bf16[384,512]{1,0:T(8,128)(2,1)}, u32[]{:S(2)}, u32[]{:S(2)}) collective-permute-start(bf16[384,512]{1,0:T(8,128)(2,1)} %get-tuple-element.69), channel_id=1, source_target_pairs={{0,32},{32,64},{64,96},{96,128},{128,160},{160,192},{192,224},{224... | collective-permute-start | bytes 1179656 | tf_op jit(solution)/shard_map/ppermute | solution.py:28
  175.6 4.8 %copy-start.14 = (f32[128]{0:T(128)S(1)}, f32[128]{0:T(128)}, u32[]{:S(2)}) copy-start(f32[128]{0:T(128)} %copy-done.13) | copy-start | bytes 1540
  179.3 0.9 copy-start
  180.1 1.0 copy-start.3
  180.2 20.7 %copy-start.1 = (f32[384,512]{1,0:T(8,128)S(1)}, f32[384,512]{1,0:T(8,128)}, u32[]{:S(2)}) copy-start(f32[384,512]{1,0:T(8,128)} %copy-done) | copy-start | bytes 2359300
  183.0 23.9 %all-to-all-start.5 = ((bf16[8,2,6144]{2,1,0:T(2,128)(2,1)}), bf16[8,2,6144]{2,1,0:T(2,128)(2,1)S(1)}, u32[]{:S(2)}, u32[]{:S(2)}) async-start(bf16[8,2,6144]{2,1,0:T(2,128)(2,1)} %reshape.220), calls=%async_computation.5 | async-start | bytes 393216 | tf_op jit(solution)/shard_map/all_to_all | solution.py:113
  206.9 11.6 %all-to-all-start.6 = ((bf16[8,2,6144]{2,1,0:T(2,128)(2,1)}), bf16[8,2,6144]{2,1,0:T(2,128)(2,1)S(1)}, u32[]{:S(2)}, u32[]{:S(2)}) async-start(bf16[8,2,6144]{2,1,0:T(2,128)(2,1)} %reshape.222), calls=%async_computation.6 | async-start | bytes 393216 | tf_op jit(solution)/shard_map/all_to_all | solution.py:116
  214.5 9.2 %copy-start.16 = (f32[128]{0:T(128)S(1)}, f32[128]{0:T(128)}, u32[]{:S(2)}) copy-start(f32[128]{0:T(128)} %get-tuple-element.65) | copy-start | bytes 1540
  218.5 126.2 %all-to-all-start.7 = ((bf16[8,2,6144]{2,1,0:T(2,128)(2,1)}), bf16[8,2,6144]{2,1,0:T(2,128)(2,1)S(1)}, u32[]{:S(2)}, u32[]{:S(2)}) async-start(bf16[8,2,6144]{2,1,0:T(2,128)(2,1)} %reshape.224), calls=%async_computation.7 | async-start | bytes 393216 | tf_op jit(solution)/shard_map/all_to_all | solution.py:119
where the time goes:
time: 352 us; the launch traced here: 346 us
  blocking collectives  119 us (34%)
  starting transfers between devices  97 us (28%)
  other arithmetic  65.5 us (19%)
  local copies, waits for them, and re-layouts  41.5 us (12%)
  waiting for transfers between devices  10.7 us (3%)
  matrix products  10.2 us (3%)
    psum x1, blocking collectives, local(): gain_total = lax.psum(gain_part, ('slab', 'head', 'dp'))  119 us
    unnamed x8, other arithmetic  55.9 us
    unnamed x66, local copies, waits for them, and re-layouts  24.6 us
    all_to_all x1, starting transfers between devices, local(): lax.all_to_all(out_tile.reshape(1, rows, width), 'head', split_axis=1, co...  19.2 us
    all_to_all x1, starting transfers between devices, local(): lax.all_to_all(q_grad.reshape(1, rows, width), 'head', split_axis=1, conc...  17.4 us
    ppermute x2, starting transfers between devices, passed_along(): lax.ppermute(value, axis, [(source, source + steps) for source in range(l...  13.7 us
    all_to_all x1, starting transfers between devices, local(): lax.all_to_all(v_proj, 'head', split_axis=2, concat_axis=1, tiled=True)  10.7 us
    ppermute x1, starting transfers between devices, with_halo(): before = lax.ppermute(last, axis, up)  8.67 us
  transfers between devices with their start and end apart: 12, of which 7 were waited for; matrix products, arithmetic and copies ran while one was open for 24% of the time, Pallas kernels for 0%

commit v1 on v0

v1 whole, which is shorter than its diff:
```python
import functools
import math

import jax
import jax.numpy as jnp
from jax import lax
from jax.experimental import pallas as pl
from jax.experimental.pallas import tpu as pltpu
from jax.sharding import PartitionSpec as P

MESH = pl.DeviceIdType.MESH
TILE = 384
HD = 128
EPS = 1e-06
SCALE = HD**-0.5
LOG2E = math.log2(math.e)
LN2 = math.log(2.0)
F32 = jnp.float32
BF16 = jnp.bfloat16


def dot(a, b, dims=((1,), (0,))):
    return lax.dot_general(a, b, (dims, ((), ())), preferred_element_type=F32)


def kernel(
    sizes,
    q_in, k_in, v_in, d_in, gains, mask,
    att_out, qg_out, kg_out, vg_out, gain_out,
    kraw, vbuf, qraw, dbuf,
    knorm, knt, vt, qs,
    kunit, krb, qunit, qrb,
    expo, dsc,
    att, qg, kg, vg,
    halo_out, halo_in,
    gring, gz, gx,
    in_send, in_recv, kv_send, kv_recv, out_send, out_recv, halo_send, halo_recv, g_send, g_recv,
):
    heads, planes, clips, total = sizes
    ring = 2 * heads
    chunk = TILE // heads
    slab = lax.axis_index("slab")
    plane = slab // 2
    side = slab % 2
    me = side * heads + lax.axis_index("head")
    clip = lax.axis_index("dp")

    def ring_id(p):
        return {"slab": 2 * plane + p // heads, "head": p % heads}

    def plane_id(z):
        return {"slab": 2 * z + side}

    def rows(p, base=0):
        return pl.ds(pl.multiple_of(base + p * chunk, 16), chunk)

    def cols(p):
        return pl.ds(pl.multiple_of(p * HD, HD), HD)

    def peer(s):
        off = jnp.where(s % 2 == 1, (s + 1) // 2, ring - s // 2)
        return lax.rem(me + off, ring)

    below = lax.rem(plane + planes - 1, planes)
    above = lax.rem(plane + 1, planes)

    barrier = pltpu.get_barrier_semaphore()

    def greet_ring(s, c):
        pl.semaphore_signal(barrier, inc=1, device_id=ring_id(peer(s)), device_id_type=MESH)
        return c

    def greet_plane(s, c):
        pl.semaphore_signal(
            barrier, inc=1, device_id=plane_id(lax.rem(plane + s, planes)), device_id_type=MESH
        )
        return c

    def greet_clip(s, c):
        pl.semaphore_signal(
            barrier, inc=1, device_id={"dp": lax.rem(clip + s, clips)}, device_id_type=MESH
        )
        return c

    lax.fori_loop(1, ring, greet_ring, 0)
    lax.fori_loop(1, planes, greet_plane, 0)
    lax.fori_loop(1, clips, greet_clip, 0)
    pl.semaphore_wait(barrier, ring - 1 + planes - 1 + clips - 1)

    arrays = ((k_in, kraw, TILE), (v_in, vbuf, TILE), (q_in, qraw, 0), (d_in, dbuf, 0))
    for i, (src, dst, base) in enumerate(arrays):
        pltpu.make_async_copy(
            src.at[0, :, cols(me)], dst.at[rows(me, base), :], in_recv.at[i, side]
        ).start()

    for i, (src, dst, base) in enumerate(arrays):

        def send_in(s, c, i=i, src=src, dst=dst, base=base):
            p = peer(s)
            pltpu.make_async_remote_copy(
                src_ref=src.at[0, :, cols(p)],
                dst_ref=dst.at[rows(me, base), :],
                send_sem=in_send.at[i],
                recv_sem=in_recv.at[i, side],
                device_id=ring_id(p),
                device_id_type=MESH,
            ).start()
            return c

        lax.fori_loop(1, ring, send_in, 0)

    def wait_bytes(ref, sem):
        pltpu.make_async_copy(ref, ref, sem).wait()

    def tile(t):
        return pl.ds(t * TILE, TILE)

    def kv_copy(i, buf, up):
        return pltpu.make_async_remote_copy(
            src_ref=buf.at[tile(2 if up else 1), :],
            dst_ref=buf.at[tile(0 if up else 3), :],
            send_sem=kv_send.at[i, up],
            recv_sem=kv_recv.at[i, up],
            device_id=plane_id(above if up else below),
            device_id_type=MESH,
        )

    kv_copies = []
    for i, buf in ((0, kraw), (1, vbuf)):
        for up in (0, 1):
            wait_bytes(buf.at[tile(1 + up), :], in_recv.at[i, up])
            copy = kv_copy(i, buf, up)
            copy.start()
            kv_copies.append(copy)

    g0 = gains[0:1, :]
    g1 = gains[1:2, :]

    def norm(raw):
        x = raw.astype(F32)
        r = lax.rsqrt(jnp.mean(x * x, axis=-1, keepdims=True) + EPS)
        return x * r, r

    def do_k(t):
        unit, r = norm(kraw[tile(t), :])
        n = unit * g1
        knorm[tile(t), :] = n.astype(BF16)
        knt[:, tile(t)] = n.T.astype(BF16)
        if t in (1, 2):
            kunit[tile(t - 1), :] = unit
            krb[tile(t - 1), :] = jnp.broadcast_to(r, unit.shape)

    def do_v(t):
        vt[:, tile(t)] = vbuf[tile(t), :].astype(F32).T.astype(BF16)

    do_k(1)
    do_k(2)
    do_v(1)
    do_v(2)
    for t, up in ((0, 1), (3, 0)):
        kv_copies[up].wait_recv()
        do_k(t)
        kv_copies[2 + up].wait_recv()
        do_v(t)

    invs = []
    outs = []
    for a in (0, 1):
        wait_bytes(qraw.at[tile(a), :], in_recv.at[2, a])
        unit, r = norm(qraw[tile(a), :])
        qunit[tile(a), :] = unit
        qrb[tile(a), :] = jnp.broadcast_to(r, unit.shape)
        qs[tile(a), :] = (unit * (g0 * (SCALE * LOG2E))).astype(BF16)
    for a in (0, 1):
        den = jnp.zeros((1, TILE), F32)
        for j in range(3):
            on = mask[0, 2 * plane + a, j].astype(F32)
            s = dot(knorm[tile(a + j), :], qs[tile(a), :], ((1,), (1,)))
            e = jnp.exp2(s) * on
            den = den + jnp.sum(e, axis=0, keepdims=True)
            expo[a, tile(j), :] = e.astype(BF16)
        inv = 1.0 / den
        out_t = (dot(vt[:, a * TILE : (a + 3) * TILE], expo[a]) * inv).astype(BF16).astype(F32)
        att[tile(a), :] = out_t.T.astype(BF16)
        invs.append(inv)
        outs.append(out_t)

    def send_out(i, buf, out, a):
        def step(p, c):
            @pl.when(p != me)
            def _():
                pltpu.make_async_remote_copy(
                    src_ref=buf.at[rows(p), :],
                    dst_ref=out.at[0, :, cols(me)],
                    send_sem=out_send.at[i],
                    recv_sem=out_recv.at[i],
                    device_id=ring_id(p),
                    device_id_type=MESH,
                ).start()

            @pl.when(p == me)
            def _():
                pltpu.make_async_copy(buf.at[rows(p), :], out.at[0, :, cols(p)], out_recv.at[i]).start()

            return c

        lax.fori_loop(a * heads, (a + 1) * heads, step, 0)

    send_out(0, att, att_out, 0)
    send_out(0, att, att_out, 1)

    def halo_copy(i, up):
        return pltpu.make_async_remote_copy(
            src_ref=halo_out.at[i, up],
            dst_ref=halo_in.at[i, up],
            send_sem=halo_send.at[i, up],
            recv_sem=halo_recv.at[i, up],
            device_id=plane_id(above if up else below),
            device_id_type=MESH,
        )

    douts = []
    doscs = []
    deltas = []
    halo_copies = {}

    def dscore(a, j):
        dp = dot(vbuf[tile(a + j), :], douts[a])
        dsc[a, tile(j), :] = (expo[a, tile(j), :].astype(F32) * (dp - deltas[a])).astype(BF16)

    for a in (0, 1):
        wait_bytes(dbuf.at[tile(a), :], in_recv.at[3, a])
        dt = dbuf[tile(a), :].astype(F32).T * invs[a]
        dtb = dt.astype(BF16)
        douts.append(dtb)
        doscs.append(dt.T.astype(BF16))
        deltas.append(jnp.sum(dtb.astype(F32) * outs[a], axis=0, keepdims=True))
        j = 2 * a
        halo_out[1, a] = dot(expo[a, tile(j), :], doscs[a]).astype(BF16)
        halo_copies[1, a] = halo_copy(1, a)
        halo_copies[1, a].start()
        dscore(a, j)
        halo_out[0, a] = (dot(dsc[a, tile(j), :], qs[tile(a), :]) * LN2).astype(BF16)
        halo_copies[0, a] = halo_copy(0, a)
        halo_copies[0, a].start()

    def norm_backward(unit, r, gain, grad):
        inner = grad * gain
        return r * (inner - unit * jnp.mean(inner * unit, axis=-1, keepdims=True))

    gain_q = jnp.zeros((1, HD), F32)
    for a in (0, 1):
        for j in range(3):
            if j != 2 * a:
                dscore(a, j)
        dq = dot(knt[:, a * TILE : (a + 3) * TILE], dsc[a]).T * SCALE
        unit = qunit[tile(a), :]
        gain_q = gain_q + jnp.sum(dq * unit, axis=0, keepdims=True)
        qg[tile(a), :] = norm_backward(unit, qrb[tile(a), :], g0, dq).astype(BF16)
        send_out(1, qg, qg_out, a)

    gain_k = jnp.zeros((1, HD), F32)
    for t in (0, 1):
        dv = dot(expo[0, tile(1 + t), :], doscs[0]) + dot(expo[1, tile(t), :], doscs[1])
        halo_copies[1, 1 - t].wait_recv()
        vg[tile(t), :] = (dv + halo_in[1, 1 - t].astype(F32)).astype(BF16)
        send_out(3, vg, vg_out, t)
        dk = dot(dsc[0, tile(1 + t), :], qs[tile(0), :]) + dot(dsc[1, tile(t), :], qs[tile(1), :])
        halo_copies[0, 1 - t].wait_recv()
        dk = dk * LN2 + halo_in[0, 1 - t].astype(F32)
        unit = kunit[tile(t), :]
        gain_k = gain_k + jnp.sum(dk * unit, axis=0, keepdims=True)
        kg[tile(t), :] = norm_backward(unit, krb[tile(t), :], g1, dk).astype(BF16)
        send_out(2, kg, kg_out, t)

    part = jnp.concatenate([gain_q, gain_k, jnp.zeros((6, HD), F32)], axis=0)
    for stage, (buf, here, count, target) in enumerate(
        (
            (gring, me, ring, ring_id),
            (gz, plane, planes, plane_id),
            (gx, clip, clips, lambda x: {"dp": x}),
        )
    ):
        buf[here] = part
        if count > 1:

            def send_gain(s, c, stage=stage, buf=buf, here=here, count=count, target=target):
                pltpu.make_async_remote_copy(
                    src_ref=buf.at[here],
                    dst_ref=buf.at[here],
                    send_sem=g_send.at[stage],
                    recv_sem=g_recv.at[stage],
                    device_id=target(lax.rem(here + s, count)),
                    device_id_type=MESH,
                ).start()
                return c

            lax.fori_loop(1, count, send_gain, 0)
            wait_bytes(buf.at[pl.ds(0, count - 1)], g_recv.at[stage])
        part = jnp.sum(buf[...], axis=0)
    gain_out[...] = part[0:2, :] * (1.0 / math.sqrt(total))

    for i in range(4):
        wait_bytes(att.at[pl.ds(0, 2 * TILE), :], out_recv.at[i])
        wait_bytes(att.at[pl.ds(0, 2 * TILE - chunk), :], out_send.at[i])
        wait_bytes(att.at[pl.ds(0, 2 * TILE - chunk), :], in_send.at[i])
    for copy in kv_copies:
        copy.wait_send()
    for copy in halo_copies.values():
        copy.wait_send()
    for stage, (buf, count) in enumerate(((gring, ring), (gz, planes), (gx, clips))):
        if count > 1:
            wait_bytes(buf.at[pl.ds(0, count - 1)], g_send.at[stage])


def solution(mesh):
    heads = mesh.shape["head"]
    planes = mesh.shape["slab"] // 2
    clips = mesh.shape["dp"]
    ring = 2 * heads
    total = clips * planes * 2 * TILE * ring
    sizes = (heads, planes, clips, total)

    def local(q_proj, k_proj, v_proj, grad_out, norm_gains, window_mask):
        hbm = pl.BlockSpec(memory_space=pltpu.HBM)
        vmem = pl.BlockSpec(memory_space=pltpu.VMEM)
        big = jax.ShapeDtypeStruct(q_proj.shape, BF16)
        dma = pltpu.SemaphoreType.DMA
        return pl.pallas_call(
            functools.partial(kernel, sizes),
            out_shape=(big, big, big, big, jax.ShapeDtypeStruct((2, HD), F32)),
            in_specs=[hbm, hbm, hbm, hbm, vmem, pl.BlockSpec(memory_space=pltpu.SMEM)],
            out_specs=(hbm, hbm, hbm, hbm, vmem),
            scratch_shapes=[
                pltpu.VMEM((4 * TILE, HD), BF16),
                pltpu.VMEM((4 * TILE, HD), BF16),
                pltpu.VMEM((2 * TILE, HD), BF16),
                pltpu.VMEM((2 * TILE, HD), BF16),
                pltpu.VMEM((4 * TILE, HD), BF16),
                pltpu.VMEM((HD, 4 * TILE), BF16),
                pltpu.VMEM((HD, 4 * TILE), BF16),
                pltpu.VMEM((2 * TILE, HD), BF16),
                pltpu.VMEM((2 * TILE, HD), F32),
                pltpu.VMEM((2 * TILE, HD), F32),
                pltpu.VMEM((2 * TILE, HD), F32),
                pltpu.VMEM((2 * TILE, HD), F32),
                pltpu.VMEM((2, 3 * TILE, TILE), BF16),
                pltpu.VMEM((2, 3 * TILE, TILE), BF16),
                pltpu.VMEM((2 * TILE, HD), BF16),
                pltpu.VMEM((2 * TILE, HD), BF16),
                pltpu.VMEM((2 * TILE, HD), BF16),
                pltpu.VMEM((2 * TILE, HD), BF16),
                pltpu.VMEM((2, 2, TILE, HD), BF16),
                pltpu.VMEM((2, 2, TILE, HD), BF16),
                pltpu.VMEM((ring, 8, HD), F32),
                pltpu.VMEM((planes, 8, HD), F32),
                pltpu.VMEM((clips, 8, HD), F32),
                dma((4,)),
                dma((4, 2)),
                dma((2, 2)),
                dma((2, 2)),
                dma((4,)),
                dma((4,)),
                dma((2, 2)),
                dma((2, 2)),
                dma((3,)),
                dma((3,)),
            ],
            compiler_params=pltpu.CompilerParams(
                collective_id=0, has_side_effects=True, vmem_limit_bytes=40 * 1024 * 1024
            ),
        )(q_proj, k_proj, v_proj, grad_out, norm_gains, window_mask)

    tokens = P("dp", ("slab", "head"), None)
    return jax.shard_map(
        local,
        mesh=mesh,
        in_specs=(tokens, tokens, tokens, tokens, P(), P("dp", None, None)),
        out_specs=(tokens, tokens, tokens, tokens, P()),
        check_vma=False,
    )
```

time: 352 us -> 73.4 us (0.21); the launches traced: 346 us -> 73.2 us
  blocking collectives: 119 us -> 0 us
  starting transfers between devices: 97 us -> 0 us
  other arithmetic: 65.5 us -> 0 us
  Pallas kernels: 0 us -> 64.8 us
  local copies, waits for them, and re-layouts: 41.5 us -> 7.74 us
  waiting for transfers between devices: 10.7 us -> 0 us
  matrix products: 10.2 us -> 0 us
    psum x1 -> x0, blocking collectives: 119 us -> none  [local(): gain_total = lax.psum(gain_part, ('slab', 'head', 'dp'))]
    all_to_all x8 -> x0, starting transfers between devices: 73.3 us -> none  [the longest x1 19.2 us: local(): lax.all_to_all(out_tile.reshape(1, rows, width), 'head', split_axis=1, co...]
    pallas_call x0 -> x1, Pallas kernels: none -> 64.8 us  [local(): pl.pallas_call(functools.partial(kernel, sizes), out_shape=(big, big, big...]
    unnamed x8 -> x0, other arithmetic: 55.9 us -> none
    ppermute x4 -> x0, starting transfers between devices: 23.7 us -> none  [the longest x2 13.7 us: passed_along(): lax.ppermute(value, axis, [(source, source + steps) for source in range(l...]
    unnamed x66 -> x16, local copies, waits for them, and re-layouts: 24.6 us -> 7.74 us
    dot_general x5 -> x0, matrix products: 7.92 us -> none  [the longest x1 2.51 us: local(): jnp.einsum('hqk,qhd->khd', prob, dout, preferred_element_type=jnp.float32)]
    all_to_all x8 -> x0, waiting for transfers between devices: 7.22 us -> none  [the longest x1 3.87 us: local(): lax.all_to_all(grad_out, 'head', split_axis=2, concat_axis=1, tiled=True)]
  transfers between devices with their start and end apart: 12 -> 0, of which waited for: 7 -> 0; matrix products, arithmetic and copies ran while one was open for 24% -> 0% of each run, Pallas kernels for 0% -> 0%
where the time goes in v1:
time: 73.4 us; the launch traced here: 73.2 us
  Pallas kernels  64.8 us (88%)
  local copies, waits for them, and re-layouts  7.74 us (11%)
    pallas_call x1, Pallas kernels, local(): pl.pallas_call(functools.partial(kernel, sizes), out_shape=(big, big, big...  64.8 us
    unnamed x16, local copies, waits for them, and re-layouts  7.74 us

profile of v1, /device:TPU:1, one launch (start us, length us, event | category | flops | bytes accessed | tf_op | source)
XLA Modules:
  0.0 73.2 jit_solution(3585319491859406864)
XLA Ops:
  0.6 0.0 copy-start.4
  0.6 0.8 %copy.11.mask = s32[1,16,3]{2,1,0:T(8,128)S(1)} copy(s32[1,16,3]{1,0,2:T(1,128)} %param.11) | data formatting | bytes 384 | tf_op args[5]
  1.4 0.0 copy-done.4
  1.4 0.0 copy-start
  1.4 0.9 %copy-done = bf16[1,48,2048]{2,1,0:T(8,128)(2,1)S(1)} copy-done((bf16[1,48,2048]{2,1,0:T(8,128)(2,1)S(1)}, bf16[1,48,2048]{2,1,0:T(8,128)(2,1)}, u32[]{:S(2)}) %copy-start) | copy-done | bytes 196632
  2.3 0.0 copy-start.1
  2.3 0.9 %copy-done.1 = bf16[1,48,2048]{2,1,0:T(8,128)(2,1)S(1)} copy-done((bf16[1,48,2048]{2,1,0:T(8,128)(2,1)S(1)}, bf16[1,48,2048]{2,1,0:T(8,128)(2,1)}, u32[]{:S(2)}) %copy-start.1) | copy-done | bytes 196632
  3.3 0.0 copy-start.2
  3.3 0.9 %copy-done.2 = bf16[1,48,2048]{2,1,0:T(8,128)(2,1)S(1)} copy-done((bf16[1,48,2048]{2,1,0:T(8,128)(2,1)S(1)}, bf16[1,48,2048]{2,1,0:T(8,128)(2,1)}, u32[]{:S(2)}) %copy-start.2) | copy-done | bytes 196632
  4.2 0.0 copy-start.3
  4.2 0.9 %copy-done.3 = bf16[1,48,2048]{2,1,0:T(8,128)(2,1)S(1)} copy-done((bf16[1,48,2048]{2,1,0:T(8,128)(2,1)S(1)}, bf16[1,48,2048]{2,1,0:T(8,128)(2,1)}, u32[]{:S(2)}) %copy-start.3) | copy-done | bytes 196632
  5.1 64.8 %shard_map.101 = (bf16[1,48,2048]{2,1,0:T(8,128)(2,1)S(1)}, bf16[1,48,2048]{2,1,0:T(8,128)(2,1)S(1)}, bf16[1,48,2048]{2,1,0:T(8,128)(2,1)S(1)}, bf16[1,48,2048]{2,1,0:T(8,128)(2,1)S(1)}, f32[2,128]{1,0:T(2,128)S(1)}) custom-call(bf16[1,48,2048]{2,1,0:T(8,128)(2,1)S(1)} %copy-done, bf16[1,48,2048]{2,1,0:T(8,128)(2,1)S(1)} %copy-done.1, ...), custom_call_target="tpu_custom_call" | custom-call | tf_op jit(solution)/shard_map/pallas_call | solution.py:329
  69.9 0.7 copy.17
  70.6 0.7 copy.18
  71.2 0.7 copy.19
  71.9 0.7 copy.20
  72.6 0.6 copy.21
Async XLA Ops:
  0.6 0.8 %copy-start.4 = (f32[2,128]{1,0:T(2,128)S(1)}, f32[2,128]{1,0:T(2,128)}, u32[]{:S(2)}) copy-start(f32[2,128]{1,0:T(2,128)} %gains.1) | copy-start | bytes 3076
  1.4 0.9 %copy-start = (bf16[1,48,2048]{2,1,0:T(8,128)(2,1)S(1)}, bf16[1,48,2048]{2,1,0:T(8,128)(2,1)}, u32[]{:S(2)}) copy-start(bf16[1,48,2048]{2,1,0:T(8,128)(2,1)} %q_in.1) | copy-start | bytes 589828
  2.3 0.9 %copy-start.1 = (bf16[1,48,2048]{2,1,0:T(8,128)(2,1)S(1)}, bf16[1,48,2048]{2,1,0:T(8,128)(2,1)}, u32[]{:S(2)}) copy-start(bf16[1,48,2048]{2,1,0:T(8,128)(2,1)} %k_in.1) | copy-start | bytes 589828
  3.3 0.9 %copy-start.2 = (bf16[1,48,2048]{2,1,0:T(8,128)(2,1)S(1)}, bf16[1,48,2048]{2,1,0:T(8,128)(2,1)}, u32[]{:S(2)}) copy-start(bf16[1,48,2048]{2,1,0:T(8,128)(2,1)} %v_in.1) | copy-start | bytes 589828
  4.2 0.9 %copy-start.3 = (bf16[1,48,2048]{2,1,0:T(8,128)(2,1)S(1)}, bf16[1,48,2048]{2,1,0:T(8,128)(2,1)}, u32[]{:S(2)}) copy-start(bf16[1,48,2048]{2,1,0:T(8,128)(2,1)} %d_in.1) | copy-start | bytes 589828

commit v2 on v1

--- a/solution.py
+++ b/solution.py
@@ -25,7 +25,7 @@
 
 def kernel(
     sizes,
-    q_in, k_in, v_in, d_in, gains, mask,
+    q_in, k_in, v_in, d_in, gains_in, mask_in,
     att_out, qg_out, kg_out, vg_out, gain_out,
     kraw, vbuf, qraw, dbuf,
     knorm, knt, vt, qs,
@@ -33,8 +33,8 @@
     expo, dsc,
     att, qg, kg, vg,
     halo_out, halo_in,
-    gring, gz, gx,
-    in_send, in_recv, kv_send, kv_recv, out_send, out_recv, halo_send, halo_recv, g_send, g_recv,
+    gring, gz, gx, gains, mask,
+    small_sem, in_send, in_recv, kv_send, kv_recv, out_send, out_recv, halo_send, halo_recv, g_send, g_recv,
 ):
     heads, planes, clips, total = sizes
     ring = 2 * heads
@@ -64,6 +64,13 @@
     below = lax.rem(plane + planes - 1, planes)
     above = lax.rem(plane + 1, planes)
 
+    small = (
+        pltpu.make_async_copy(gains_in, gains, small_sem.at[0]),
+        pltpu.make_async_copy(mask_in, mask, small_sem.at[1]),
+    )
+    for copy in small:
+        copy.start()
+
     barrier = pltpu.get_barrier_semaphore()
 
     def greet_ring(s, c):
@@ -93,9 +100,10 @@
             src.at[0, :, cols(me)], dst.at[rows(me, base), :], in_recv.at[i, side]
         ).start()
 
-    for i, (src, dst, base) in enumerate(arrays):
-
-        def send_in(s, c, i=i, src=src, dst=dst, base=base):
+    def send_in(i):
+        src, dst, base = arrays[i]
+
+        def step(s, c):
             p = peer(s)
             pltpu.make_async_remote_copy(
                 src_ref=src.at[0, :, cols(p)],
@@ -107,7 +115,10 @@
             ).start()
             return c
 
-        lax.fori_loop(1, ring, send_in, 0)
+        lax.fori_loop(1, ring, step, 0)
+
+    send_in(0)
+    send_in(1)
 
     def wait_bytes(ref, sem):
         pltpu.make_async_copy(ref, ref, sem).wait()
@@ -132,7 +143,10 @@
             copy = kv_copy(i, buf, up)
             copy.start()
             kv_copies.append(copy)
-
+        send_in(2 + i)
+
+    for copy in small:
+        copy.wait()
     g0 = gains[0:1, :]
     g1 = gains[1:2, :]
 
@@ -174,7 +188,7 @@
     for a in (0, 1):
         den = jnp.zeros((1, TILE), F32)
         for j in range(3):
-            on = mask[0, 2 * plane + a, j].astype(F32)
+            on = mask[j, 0, 2 * plane + a].astype(F32)
             s = dot(knorm[tile(a + j), :], qs[tile(a), :], ((1,), (1,)))
             e = jnp.exp2(s) * on
             den = den + jnp.sum(e, axis=0, keepdims=True)
@@ -186,7 +200,9 @@
         outs.append(out_t)
 
     def send_out(i, buf, out, a):
-        def step(p, c):
+        def step(s, c):
+            p = a * heads + lax.rem(me + s, heads)
+
             @pl.when(p != me)
             def _():
                 pltpu.make_async_remote_copy(
@@ -204,7 +220,7 @@
 
             return c
 
-        lax.fori_loop(a * heads, (a + 1) * heads, step, 0)
+        lax.fori_loop(0, heads, step, 0)
 
     send_out(0, att, att_out, 0)
     send_out(0, att, att_out, 1)
@@ -261,44 +277,53 @@
 
     gain_k = jnp.zeros((1, HD), F32)
     for t in (0, 1):
-        dv = dot(expo[0, tile(1 + t), :], doscs[0]) + dot(expo[1, tile(t), :], doscs[1])
-        halo_copies[1, 1 - t].wait_recv()
-        vg[tile(t), :] = (dv + halo_in[1, 1 - t].astype(F32)).astype(BF16)
-        send_out(3, vg, vg_out, t)
         dk = dot(dsc[0, tile(1 + t), :], qs[tile(0), :]) + dot(dsc[1, tile(t), :], qs[tile(1), :])
         halo_copies[0, 1 - t].wait_recv()
         dk = dk * LN2 + halo_in[0, 1 - t].astype(F32)
         unit = kunit[tile(t), :]
         gain_k = gain_k + jnp.sum(dk * unit, axis=0, keepdims=True)
         kg[tile(t), :] = norm_backward(unit, krb[tile(t), :], g1, dk).astype(BF16)
-        send_out(2, kg, kg_out, t)
-
-    part = jnp.concatenate([gain_q, gain_k, jnp.zeros((6, HD), F32)], axis=0)
-    for stage, (buf, here, count, target) in enumerate(
-        (
-            (gring, me, ring, ring_id),
-            (gz, plane, planes, plane_id),
-            (gx, clip, clips, lambda x: {"dp": x}),
-        )
-    ):
+
+    stages = (
+        (gring, me, ring, ring_id),
+        (gz, plane, planes, plane_id),
+        (gx, clip, clips, lambda x: {"dp": x}),
+    )
+
+    def gain_start(stage, part):
+        buf, here, count, target = stages[stage]
         buf[here] = part
+
+        def step(s, c):
+            pltpu.make_async_remote_copy(
+                src_ref=buf.at[here],
+                dst_ref=buf.at[here],
+                send_sem=g_send.at[stage],
+                recv_sem=g_recv.at[stage],
+                device_id=target(lax.rem(here + s, count)),
+                device_id_type=MESH,
+            ).start()
+            return c
+
+        lax.fori_loop(1, count, step, 0)
+
+    def gain_end(stage):
+        buf, _, count, _ = stages[stage]
         if count > 1:
-
-            def send_gain(s, c, stage=stage, buf=buf, here=here, count=count, target=target):
-                pltpu.make_async_remote_copy(
-                    src_ref=buf.at[here],
-                    dst_ref=buf.at[here],
-                    send_sem=g_send.at[stage],
-                    recv_sem=g_recv.at[stage],
-                    device_id=target(lax.rem(here + s, count)),
-                    device_id_type=MESH,
-                ).start()
-                return c
-
-            lax.fori_loop(1, count, send_gain, 0)
             wait_bytes(buf.at[pl.ds(0, count - 1)], g_recv.at[stage])
-        part = jnp.sum(buf[...], axis=0)
-    gain_out[...] = part[0:2, :] * (1.0 / math.sqrt(total))
+        return jnp.sum(buf[...], axis=0)
+
+    gain_start(0, jnp.concatenate([gain_q, gain_k, jnp.zeros((6, HD), F32)], axis=0))
+    for t in (0, 1):
+        dv = dot(expo[0, tile(1 + t), :], doscs[0]) + dot(expo[1, tile(t), :], doscs[1])
+        halo_copies[1, 1 - t].wait_recv()
+        vg[tile(t), :] = (dv + halo_in[1, 1 - t].astype(F32)).astype(BF16)
+        send_out(3, vg, vg_out, t)
+    gain_start(1, gain_end(0))
+    send_out(2, kg, kg_out, 0)
+    gain_start(2, gain_end(1))
+    send_out(2, kg, kg_out, 1)
+    gain_out[...] = gain_end(2)[0:2, :] * (1.0 / math.sqrt(total))
 
     for i in range(4):
         wait_bytes(att.at[pl.ds(0, 2 * TILE), :], out_recv.at[i])
@@ -313,6 +338,15 @@
             wait_bytes(buf.at[pl.ds(0, count - 1)], g_send.at[stage])
 
 
+def store(*refs):
+    sems = refs[10]
+    copies = [pltpu.make_async_copy(refs[i], refs[5 + i], sems.at[i]) for i in range(5)]
+    for copy in copies:
+        copy.start()
+    for copy in copies:
+        copy.wait()
+
+
 def solution(mesh):
     heads = mesh.shape["head"]
     planes = mesh.shape["slab"] // 2
@@ -325,12 +359,15 @@
         hbm = pl.BlockSpec(memory_space=pltpu.HBM)
         vmem = pl.BlockSpec(memory_space=pltpu.VMEM)
         big = jax.ShapeDtypeStruct(q_proj.shape, BF16)
+        outs_shape = (big, big, big, big, jax.ShapeDtypeStruct((2, HD), F32))
+        landing = tuple(pltpu.VMEM(x.shape, x.dtype) for x in outs_shape)
+        operands = (q_proj, k_proj, v_proj, grad_out, norm_gains, jnp.transpose(window_mask, (2, 0, 1)))
         dma = pltpu.SemaphoreType.DMA
-        return pl.pallas_call(
+        outs = pl.pallas_call(
             functools.partial(kernel, sizes),
-            out_shape=(big, big, big, big, jax.ShapeDtypeStruct((2, HD), F32)),
-            in_specs=[hbm, hbm, hbm, hbm, vmem, pl.BlockSpec(memory_space=pltpu.SMEM)],
-            out_specs=(hbm, hbm, hbm, hbm, vmem),
+            out_shape=landing,
+            in_specs=[hbm] * 6,
+            out_specs=(vmem,) * 5,
             scratch_shapes=[
                 pltpu.VMEM((4 * TILE, HD), BF16),
                 pltpu.VMEM((4 * TILE, HD), BF16),
@@ -355,6 +392,9 @@
                 pltpu.VMEM((ring, 8, HD), F32),
                 pltpu.VMEM((planes, 8, HD), F32),
                 pltpu.VMEM((clips, 8, HD), F32),
+                pltpu.VMEM((2, HD), F32),
+                pltpu.SMEM((3, 1, 2 * planes), jnp.int32),
+                dma((2,)),
                 dma((4,)),
                 dma((4, 2)),
                 dma((2, 2)),
@@ -369,7 +409,14 @@
             compiler_params=pltpu.CompilerParams(
                 collective_id=0, has_side_effects=True, vmem_limit_bytes=40 * 1024 * 1024
             ),
-        )(q_proj, k_proj, v_proj, grad_out, norm_gains, window_mask)
+        )(*(pltpu.with_memory_space_constraint(x, pltpu.HBM) for x in operands))
+        return pl.pallas_call(
+            store,
+            out_shape=outs_shape,
+            in_specs=[vmem] * 5,
+            out_specs=(hbm,) * 5,
+            scratch_shapes=[dma((5,))],
+        )(*outs)
 
     tokens = P("dp", ("slab", "head"), None)
     return jax.shard_map(

time: 73.4 us -> 65 us (0.89)
  local copies, waits for them, and re-layouts: 7.74 us -> 3.26 us
  Pallas kernels: 64.8 us -> 60.5 us
    unnamed x16 -> x10, local copies, waits for them, and re-layouts: 7.74 us -> 3.26 us
    pallas_call x1 -> x2, Pallas kernels: 64.8 us -> 60.5 us  [the longest x1 58.3 us: local(): pl.pallas_call(functools.partial(kernel, sizes), out_shape=landing, in_sp...]
where the time goes in v2:
time: 65 us; the launch traced here: 64.4 us
  Pallas kernels  60.5 us (93%)
  local copies, waits for them, and re-layouts  3.26 us (5%)
  between operations  0.65 us (1%)
    pallas_call x1, Pallas kernels, local(): pl.pallas_call(functools.partial(kernel, sizes), out_shape=landing, in_sp...  58.3 us
    unnamed x10, local copies, waits for them, and re-layouts  3.26 us
    pallas_call x1, Pallas kernels, local(): pl.pallas_call(store, out_shape=outs_shape, in_specs=[vmem] * 5, out_spec...  2.13 us

profile of v2, /device:TPU:1, one launch (start us, length us, event | category | flops | bytes accessed | tf_op | source)
XLA Modules:
  0.0 64.4 jit_solution(6023034282248715453)
XLA Ops:
  0.6 58.3 %shard_map.101 = (bf16[1,48,2048]{2,1,0:T(8,128)(2,1)S(1)}, bf16[1,48,2048]{2,1,0:T(8,128)(2,1)S(1)}, bf16[1,48,2048]{2,1,0:T(8,128)(2,1)S(1)}, bf16[1,48,2048]{2,1,0:T(8,128)(2,1)S(1)}, f32[2,128]{1,0:T(2,128)S(1)}) custom-call(bf16[1,48,2048]{2,1,0:T(8,128)(2,1)} %q_in.1, bf16[1,48,2048]{2,1,0:T(8,128)(2,1)} %k_in.1, bf16[1,48,2048]{2,1,0:T(8,128)(2,1)} %v_in.1, ...), custom_call_target="tpu_custom_call" | custom-call | tf_op jit(solution)/shard_map/pallas_call | solution.py:366
  59.0 0.0 copy-start
  59.0 0.7 %copy-done = bf16[1,48,2048]{2,1,0:T(8,128)(2,1)} copy-done((bf16[1,48,2048]{2,1,0:T(8,128)(2,1)}, bf16[1,48,2048]{2,1,0:T(8,128)(2,1)S(1)}, u32[]{:S(2)}) %copy-start) | copy-done | bytes 196632
  59.7 0.0 copy-start.1
  59.7 0.7 %copy-done.1 = bf16[1,48,2048]{2,1,0:T(8,128)(2,1)} copy-done((bf16[1,48,2048]{2,1,0:T(8,128)(2,1)}, bf16[1,48,2048]{2,1,0:T(8,128)(2,1)S(1)}, u32[]{:S(2)}) %copy-start.1) | copy-done | bytes 196632
  60.3 0.0 copy-start.2
  60.3 0.7 %copy-done.2 = bf16[1,48,2048]{2,1,0:T(8,128)(2,1)} copy-done((bf16[1,48,2048]{2,1,0:T(8,128)(2,1)}, bf16[1,48,2048]{2,1,0:T(8,128)(2,1)S(1)}, u32[]{:S(2)}) %copy-start.2) | copy-done | bytes 196632
  61.0 0.0 copy-start.3
  61.0 0.7 %copy-done.3 = bf16[1,48,2048]{2,1,0:T(8,128)(2,1)} copy-done((bf16[1,48,2048]{2,1,0:T(8,128)(2,1)}, bf16[1,48,2048]{2,1,0:T(8,128)(2,1)S(1)}, u32[]{:S(2)}) %copy-start.3) | copy-done | bytes 196632
  61.7 0.0 copy-start.4
  61.7 0.6 copy-done.4
  62.3 2.1 %shard_map.102 = (bf16[1,48,2048]{2,1,0:T(8,128)(2,1)}, bf16[1,48,2048]{2,1,0:T(8,128)(2,1)}, bf16[1,48,2048]{2,1,0:T(8,128)(2,1)}, bf16[1,48,2048]{2,1,0:T(8,128)(2,1)}, f32[2,128]{1,0:T(2,128)}) custom-call(bf16[1,48,2048]{2,1,0:T(8,128)(2,1)} %copy-done, bf16[1,48,2048]{2,1,0:T(8,128)(2,1)} %copy-done.1, bf16[1,48,2048]{2,1,0:T(8,128)(2,1)} %copy-done.2, ...), custom_call_target="tpu_custom_call" | custom-call | tf_op jit(solution)/shard_map/pallas_call | solution.py:413
Async XLA Ops:
  59.0 0.7 %copy-start = (bf16[1,48,2048]{2,1,0:T(8,128)(2,1)}, bf16[1,48,2048]{2,1,0:T(8,128)(2,1)S(1)}, u32[]{:S(2)}) copy-start(bf16[1,48,2048]{2,1,0:T(8,128)(2,1)S(1)} %get-tuple-element.10.refs_0_) | copy-start | bytes 589828
  59.7 0.7 %copy-start.1 = (bf16[1,48,2048]{2,1,0:T(8,128)(2,1)}, bf16[1,48,2048]{2,1,0:T(8,128)(2,1)S(1)}, u32[]{:S(2)}) copy-start(bf16[1,48,2048]{2,1,0:T(8,128)(2,1)S(1)} %get-tuple-element.11.refs_1_) | copy-start | bytes 589828
  60.3 0.7 %copy-start.2 = (bf16[1,48,2048]{2,1,0:T(8,128)(2,1)}, bf16[1,48,2048]{2,1,0:T(8,128)(2,1)S(1)}, u32[]{:S(2)}) copy-start(bf16[1,48,2048]{2,1,0:T(8,128)(2,1)S(1)} %get-tuple-element.12.refs_2_) | copy-start | bytes 589828
  61.0 0.7 %copy-start.3 = (bf16[1,48,2048]{2,1,0:T(8,128)(2,1)}, bf16[1,48,2048]{2,1,0:T(8,128)(2,1)S(1)}, u32[]{:S(2)}) copy-start(bf16[1,48,2048]{2,1,0:T(8,128)(2,1)S(1)} %get-tuple-element.13.refs_3_) | copy-start | bytes 589828
  61.7 0.6 copy-start.4

commit v3 on v2

--- a/solution.py
+++ b/solution.py
@@ -28,11 +28,11 @@
     q_in, k_in, v_in, d_in, gains_in, mask_in,
     att_out, qg_out, kg_out, vg_out, gain_out,
     kraw, vbuf, qraw, dbuf,
-    knorm, knt, vt, qs,
+    knorm, knt, vt, qs, qst,
     kunit, krb, qunit, qrb,
     expo, dsc,
     att, qg, kg, vg,
-    halo_out, halo_in,
+    halo_out, halo_in, den, out_t, dout_t, dout_s, delta,
     gring, gz, gx, gains, mask,
     small_sem, in_send, in_recv, kv_send, kv_recv, out_send, out_recv, halo_send, halo_recv, g_send, g_recv,
 ):
@@ -40,13 +40,13 @@
     ring = 2 * heads
     chunk = TILE // heads
     slab = lax.axis_index("slab")
-    plane = slab // 2
-    side = slab % 2
+    plane = lax.div(slab, 2)
+    side = lax.rem(slab, 2)
     me = side * heads + lax.axis_index("head")
     clip = lax.axis_index("dp")
 
     def ring_id(p):
-        return {"slab": 2 * plane + p // heads, "head": p % heads}
+        return {"slab": 2 * plane + lax.div(p, heads), "head": lax.rem(p, heads)}
 
     def plane_id(z):
         return {"slab": 2 * z + side}
@@ -58,7 +58,8 @@
         return pl.ds(pl.multiple_of(p * HD, HD), HD)
 
     def peer(s):
-        off = jnp.where(s % 2 == 1, (s + 1) // 2, ring - s // 2)
+        half = lax.div(s + 1, 2)
+        off = jnp.where(lax.rem(s, 2) == 1, half, ring - half)
         return lax.rem(me + off, ring)
 
     below = lax.rem(plane + planes - 1, planes)
@@ -94,7 +95,7 @@
     lax.fori_loop(1, clips, greet_clip, 0)
     pl.semaphore_wait(barrier, ring - 1 + planes - 1 + clips - 1)
 
-    arrays = ((k_in, kraw, TILE), (v_in, vbuf, TILE), (q_in, qraw, 0), (d_in, dbuf, 0))
+    arrays = ((k_in, kraw, TILE), (q_in, qraw, 0), (v_in, vbuf, TILE), (d_in, dbuf, 0))
     for i, (src, dst, base) in enumerate(arrays):
         pltpu.make_async_copy(
             src.at[0, :, cols(me)], dst.at[rows(me, base), :], in_recv.at[i, side]
@@ -124,29 +125,34 @@
         pltpu.make_async_copy(ref, ref, sem).wait()
 
     def tile(t):
-        return pl.ds(t * TILE, TILE)
-
-    def kv_copy(i, buf, up):
+        return pl.ds(pl.multiple_of(t * TILE, TILE), TILE)
+
+    def kv_copy(i, up):
+        buf = (kraw, vbuf)[i]
         return pltpu.make_async_remote_copy(
-            src_ref=buf.at[tile(2 if up else 1), :],
-            dst_ref=buf.at[tile(0 if up else 3), :],
+            src_ref=buf.at[tile(1 + up), :],
+            dst_ref=buf.at[tile(3 - 3 * up), :],
             send_sem=kv_send.at[i, up],
             recv_sem=kv_recv.at[i, up],
-            device_id=plane_id(above if up else below),
+            device_id=plane_id(jnp.where(up == 1, above, below)),
             device_id_type=MESH,
         )
 
-    kv_copies = []
-    for i, buf in ((0, kraw), (1, vbuf)):
-        for up in (0, 1):
-            wait_bytes(buf.at[tile(1 + up), :], in_recv.at[i, up])
-            copy = kv_copy(i, buf, up)
-            copy.start()
-            kv_copies.append(copy)
-        send_in(2 + i)
-
+    def each(count, body):
+        lax.fori_loop(0, count, lambda n, c: (body(n), c)[1], 0)
+
+    def forward_kv(i, arr):
+        def step(up):
+            wait_bytes((kraw, vbuf)[i].at[tile(1 + up), :], in_recv.at[arr, up])
+            kv_copy(i, up).start()
+
+        each(2, step)
+
+    forward_kv(0, 0)
+    send_in(2)
     for copy in small:
         copy.wait()
+
     g0 = gains[0:1, :]
     g1 = gains[1:2, :]
 
@@ -159,45 +165,54 @@
         unit, r = norm(kraw[tile(t), :])
         n = unit * g1
         knorm[tile(t), :] = n.astype(BF16)
-        knt[:, tile(t)] = n.T.astype(BF16)
-        if t in (1, 2):
-            kunit[tile(t - 1), :] = unit
-            krb[tile(t - 1), :] = jnp.broadcast_to(r, unit.shape)
-
-    def do_v(t):
-        vt[:, tile(t)] = vbuf[tile(t), :].astype(F32).T.astype(BF16)
-
-    do_k(1)
-    do_k(2)
-    do_v(1)
-    do_v(2)
-    for t, up in ((0, 1), (3, 0)):
-        kv_copies[up].wait_recv()
-        do_k(t)
-        kv_copies[2 + up].wait_recv()
-        do_v(t)
-
-    invs = []
-    outs = []
-    for a in (0, 1):
-        wait_bytes(qraw.at[tile(a), :], in_recv.at[2, a])
+        knt[t] = n.T.astype(BF16)
+        return unit, r
+
+    def own_k(t):
+        unit, r = do_k(t + 1)
+        kunit[tile(t), :] = unit
+        krb[tile(t), :] = jnp.broadcast_to(r, unit.shape)
+
+    def own_q(a):
+        wait_bytes(qraw.at[tile(a), :], in_recv.at[1, a])
         unit, r = norm(qraw[tile(a), :])
         qunit[tile(a), :] = unit
         qrb[tile(a), :] = jnp.broadcast_to(r, unit.shape)
-        qs[tile(a), :] = (unit * (g0 * (SCALE * LOG2E))).astype(BF16)
-    for a in (0, 1):
-        den = jnp.zeros((1, TILE), F32)
-        for j in range(3):
-            on = mask[j, 0, 2 * plane + a].astype(F32)
-            s = dot(knorm[tile(a + j), :], qs[tile(a), :], ((1,), (1,)))
-            e = jnp.exp2(s) * on
-            den = den + jnp.sum(e, axis=0, keepdims=True)
-            expo[a, tile(j), :] = e.astype(BF16)
-        inv = 1.0 / den
-        out_t = (dot(vt[:, a * TILE : (a + 3) * TILE], expo[a]) * inv).astype(BF16).astype(F32)
-        att[tile(a), :] = out_t.T.astype(BF16)
-        invs.append(inv)
-        outs.append(out_t)
+        n = unit * (g0 * (SCALE * LOG2E))
+        qs[tile(a), :] = n.astype(BF16)
+        qst[a] = n.T.astype(BF16)
+        den[a] = jnp.zeros((1, TILE), F32)
+
+    def score(a, j):
+        on = mask[j, 0, 2 * plane + a].astype(F32)
+        e = jnp.exp2(dot(knorm[tile(a + j), :], qst[a])) * on
+        den[a] = den[a] + jnp.sum(e, axis=0, keepdims=True)
+        expo[a, tile(j), :] = e.astype(BF16)
+
+    def own_score(n):
+        a = lax.div(n, 2)
+        score(a, lax.rem(n, 2) + 1 - a)
+
+    def halo_score(u):
+        kv_copy(0, 1 - u).wait_recv()
+        do_k(3 * u)
+        score(u, 2 * u)
+
+    def do_v(t):
+        vt[t] = vbuf[tile(t), :].astype(F32).T.astype(BF16)
+
+    def halo_v(u):
+        kv_copy(1, 1 - u).wait_recv()
+        do_v(3 * u)
+
+    each(2, own_k)
+    each(2, own_q)
+    send_in(3)
+    each(4, own_score)
+    each(2, halo_score)
+    forward_kv(1, 2)
+    each(2, lambda t: do_v(t + 1))
+    each(2, halo_v)
 
     def send_out(i, buf, out, a):
         def step(s, c):
@@ -222,8 +237,18 @@
 
         lax.fori_loop(0, heads, step, 0)
 
-    send_out(0, att, att_out, 0)
-    send_out(0, att, att_out, 1)
+    def forward(a):
+        total_t = dot(vt[a], expo[a, 0:TILE, :])
+        for j in (1, 2):
+            total_t = total_t + dot(vt[a + j], expo[a, j * TILE : (j + 1) * TILE, :])
+        inv = 1.0 / den[a]
+        den[a] = inv
+        rounded = (total_t * inv).astype(BF16).astype(F32)
+        out_t[a] = rounded
+        att[tile(a), :] = rounded.T.astype(BF16)
+        send_out(0, att, att_out, a)
+
+    each(2, forward)
 
     def halo_copy(i, up):
         return pltpu.make_async_remote_copy(
@@ -231,58 +256,54 @@
             dst_ref=halo_in.at[i, up],
             send_sem=halo_send.at[i, up],
             recv_sem=halo_recv.at[i, up],
-            device_id=plane_id(above if up else below),
+            device_id=plane_id(jnp.where(up == 1, above, below)),
             device_id_type=MESH,
         )
 
-    douts = []
-    doscs = []
-    deltas = []
-    halo_copies = {}
-
     def dscore(a, j):
-        dp = dot(vbuf[tile(a + j), :], douts[a])
-        dsc[a, tile(j), :] = (expo[a, tile(j), :].astype(F32) * (dp - deltas[a])).astype(BF16)
-
-    for a in (0, 1):
-        wait_bytes(dbuf.at[tile(a), :], in_recv.at[3, a])
-        dt = dbuf[tile(a), :].astype(F32).T * invs[a]
-        dtb = dt.astype(BF16)
-        douts.append(dtb)
-        doscs.append(dt.T.astype(BF16))
-        deltas.append(jnp.sum(dtb.astype(F32) * outs[a], axis=0, keepdims=True))
-        j = 2 * a
-        halo_out[1, a] = dot(expo[a, tile(j), :], doscs[a]).astype(BF16)
-        halo_copies[1, a] = halo_copy(1, a)
-        halo_copies[1, a].start()
-        dscore(a, j)
-        halo_out[0, a] = (dot(dsc[a, tile(j), :], qs[tile(a), :]) * LN2).astype(BF16)
-        halo_copies[0, a] = halo_copy(0, a)
-        halo_copies[0, a].start()
+        dp = dot(vbuf[tile(a + j), :], dout_t[a])
+        dsc[a, tile(j), :] = (expo[a, tile(j), :].astype(F32) * (dp - delta[a])).astype(BF16)
 
     def norm_backward(unit, r, gain, grad):
         inner = grad * gain
         return r * (inner - unit * jnp.mean(inner * unit, axis=-1, keepdims=True))
 
-    gain_q = jnp.zeros((1, HD), F32)
-    for a in (0, 1):
-        for j in range(3):
-            if j != 2 * a:
-                dscore(a, j)
-        dq = dot(knt[:, a * TILE : (a + 3) * TILE], dsc[a]).T * SCALE
+    def backward(a, gain):
+        wait_bytes(dbuf.at[tile(a), :], in_recv.at[3, a])
+        dt = dbuf[tile(a), :].astype(F32).T * den[a]
+        dtb = dt.astype(BF16)
+        dout_t[a] = dtb
+        dout_s[a] = dt.T.astype(BF16)
+        delta[a] = jnp.sum(dtb.astype(F32) * out_t[a], axis=0, keepdims=True)
+        far = tile(2 * a)
+        halo_out[1, a] = dot(expo[a, far, :], dout_s[a]).astype(BF16)
+        halo_copy(1, a).start()
+        each(3, lambda j: dscore(a, j))
+        halo_out[0, a] = (dot(dsc[a, far, :], qs[tile(a), :]) * LN2).astype(BF16)
+        halo_copy(0, a).start()
+        dq_t = dot(knt[a], dsc[a, 0:TILE, :])
+        for j in (1, 2):
+            dq_t = dq_t + dot(knt[a + j], dsc[a, j * TILE : (j + 1) * TILE, :])
+        dq = dq_t.T * SCALE
         unit = qunit[tile(a), :]
-        gain_q = gain_q + jnp.sum(dq * unit, axis=0, keepdims=True)
         qg[tile(a), :] = norm_backward(unit, qrb[tile(a), :], g0, dq).astype(BF16)
         send_out(1, qg, qg_out, a)
-
-    gain_k = jnp.zeros((1, HD), F32)
-    for t in (0, 1):
+        return gain + jnp.sum(dq * unit, axis=0, keepdims=True)
+
+    gain_q = lax.fori_loop(0, 2, backward, jnp.zeros((1, HD), F32))
+
+    def finish(t, gain):
+        dv = dot(expo[0, tile(1 + t), :], dout_s[0]) + dot(expo[1, tile(t), :], dout_s[1])
+        halo_copy(1, 1 - t).wait_recv()
+        vg[tile(t), :] = (dv + halo_in[1, 1 - t].astype(F32)).astype(BF16)
         dk = dot(dsc[0, tile(1 + t), :], qs[tile(0), :]) + dot(dsc[1, tile(t), :], qs[tile(1), :])
-        halo_copies[0, 1 - t].wait_recv()
+        halo_copy(0, 1 - t).wait_recv()
         dk = dk * LN2 + halo_in[0, 1 - t].astype(F32)
         unit = kunit[tile(t), :]
-        gain_k = gain_k + jnp.sum(dk * unit, axis=0, keepdims=True)
         kg[tile(t), :] = norm_backward(unit, krb[tile(t), :], g1, dk).astype(BF16)
+        return gain + jnp.sum(dk * unit, axis=0, keepdims=True)
+
+    gain_k = lax.fori_loop(0, 2, finish, jnp.zeros((1, HD), F32))
 
     stages = (
         (gring, me, ring, ring_id),
@@ -314,11 +335,7 @@
         return jnp.sum(buf[...], axis=0)
 
     gain_start(0, jnp.concatenate([gain_q, gain_k, jnp.zeros((6, HD), F32)], axis=0))
-    for t in (0, 1):
-        dv = dot(expo[0, tile(1 + t), :], doscs[0]) + dot(expo[1, tile(t), :], doscs[1])
-        halo_copies[1, 1 - t].wait_recv()
-        vg[tile(t), :] = (dv + halo_in[1, 1 - t].astype(F32)).astype(BF16)
-        send_out(3, vg, vg_out, t)
+    each(2, lambda t: send_out(3, vg, vg_out, t))
     gain_start(1, gain_end(0))
     send_out(2, kg, kg_out, 0)
     gain_start(2, gain_end(1))
@@ -329,10 +346,10 @@
         wait_bytes(att.at[pl.ds(0, 2 * TILE), :], out_recv.at[i])
         wait_bytes(att.at[pl.ds(0, 2 * TILE - chunk), :], out_send.at[i])
         wait_bytes(att.at[pl.ds(0, 2 * TILE - chunk), :], in_send.at[i])
-    for copy in kv_copies:
-        copy.wait_send()
-    for copy in halo_copies.values():
-        copy.wait_send()
+    for i in range(2):
+        for up in range(2):
+            kv_copy(i, up).wait_send()
+            halo_copy(i, up).wait_send()
     for stage, (buf, count) in enumerate(((gring, ring), (gz, planes), (gx, clips))):
         if count > 1:
             wait_bytes(buf.at[pl.ds(0, count - 1)], g_send.at[stage])
@@ -374,9 +391,10 @@
                 pltpu.VMEM((2 * TILE, HD), BF16),
                 pltpu.VMEM((2 * TILE, HD), BF16),
                 pltpu.VMEM((4 * TILE, HD), BF16),
-                pltpu.VMEM((HD, 4 * TILE), BF16),
-                pltpu.VMEM((HD, 4 * TILE), BF16),
-                pltpu.VMEM((2 * TILE, HD), BF16),
+                pltpu.VMEM((4, HD, TILE), BF16),
+                pltpu.VMEM((4, HD, TILE), BF16),
+                pltpu.VMEM((2 * TILE, HD), BF16),
+                pltpu.VMEM((2, HD, TILE), BF16),
                 pltpu.VMEM((2 * TILE, HD), F32),
                 pltpu.VMEM((2 * TILE, HD), F32),
                 pltpu.VMEM((2 * TILE, HD), F32),
@@ -389,6 +407,11 @@
                 pltpu.VMEM((2 * TILE, HD), BF16),
                 pltpu.VMEM((2, 2, TILE, HD), BF16),
                 pltpu.VMEM((2, 2, TILE, HD), BF16),
+                pltpu.VMEM((2, 1, TILE), F32),
+                pltpu.VMEM((2, HD, TILE), F32),
+                pltpu.VMEM((2, HD, TILE), BF16),
+                pltpu.VMEM((2, TILE, HD), BF16),
+                pltpu.VMEM((2, 1, TILE), F32),
                 pltpu.VMEM((ring, 8, HD), F32),
                 pltpu.VMEM((planes, 8, HD), F32),
                 pltpu.VMEM((clips, 8, HD), F32),
@@ -416,7 +439,8 @@
             in_specs=[vmem] * 5,
             out_specs=(hbm,) * 5,
             scratch_shapes=[dma((5,))],
-        )(*outs)
+            compiler_params=pltpu.CompilerParams(vmem_limit_bytes=4 * 1024 * 1024),
+        )(*(pltpu.with_memory_space_constraint(x, pltpu.VMEM) for x in outs))
 
     tokens = P("dp", ("slab", "head"), None)
     return jax.shard_map(

time: 65 us -> 63.1 us (0.971)
  local copies, waits for them, and re-layouts: 3.26 us -> 0 us
  Pallas kernels: 60.5 us -> 62.4 us
    unnamed x10 -> x0, local copies, waits for them, and re-layouts: 3.26 us -> none
    pallas_call x1, Pallas kernels: 58.3 us -> 61.5 us  [local(): pl.pallas_call(functools.partial(kernel, sizes), out_shape=landing, in_sp...]
    pallas_call x1, Pallas kernels: 2.13 us -> 0.92 us  [local(): pl.pallas_call(store, out_shape=outs_shape, in_specs=[vmem] * 5, out_spec...]
where the time goes in v3:
time: 63.1 us; the launch traced here: 63 us
  Pallas kernels  62.4 us (99%)
  between operations  0.64 us (1%)
    pallas_call x1, Pallas kernels, local(): pl.pallas_call(functools.partial(kernel, sizes), out_shape=landing, in_sp...  61.5 us

profile of v3, /device:TPU:1, one launch (start us, length us, event | category | flops | bytes accessed | tf_op | source)
XLA Modules:
  0.0 63.0 jit_solution(18429179542551578711)
XLA Ops:
  0.6 61.5 %shard_map.101 = (bf16[1,48,2048]{2,1,0:T(8,128)(2,1)S(1)}, bf16[1,48,2048]{2,1,0:T(8,128)(2,1)S(1)}, bf16[1,48,2048]{2,1,0:T(8,128)(2,1)S(1)}, bf16[1,48,2048]{2,1,0:T(8,128)(2,1)S(1)}, f32[2,128]{1,0:T(2,128)S(1)}) custom-call(bf16[1,48,2048]{2,1,0:T(8,128)(2,1)} %q_in.1, bf16[1,48,2048]{2,1,0:T(8,128)(2,1)} %k_in.1, bf16[1,48,2048]{2,1,0:T(8,128)(2,1)} %v_in.1, ...), custom_call_target="tpu_custom_call" | custom-call | tf_op jit(solution)/shard_map/pallas_call | solution.py:383
  62.1 0.9 %shard_map.102 = (bf16[1,48,2048]{2,1,0:T(8,128)(2,1)}, bf16[1,48,2048]{2,1,0:T(8,128)(2,1)}, bf16[1,48,2048]{2,1,0:T(8,128)(2,1)}, bf16[1,48,2048]{2,1,0:T(8,128)(2,1)}, f32[2,128]{1,0:T(2,128)}) custom-call(bf16[1,48,2048]{2,1,0:T(8,128)(2,1)S(1)} %get-tuple-element.10.refs_0_, bf16[1,48,2048]{2,1,0:T(8,128)(2,1)S(1)} %get-tuple-element.11.refs_1_, ...), custom_call_target="tpu_custom_call" | custom-call | tf_op jit(solution)/shard_map/pallas_call | solution.py:436

commit v4 on v2

--- a/solution.py
+++ b/solution.py
@@ -40,13 +40,13 @@
     ring = 2 * heads
     chunk = TILE // heads
     slab = lax.axis_index("slab")
-    plane = slab // 2
-    side = slab % 2
+    plane = lax.div(slab, 2)
+    side = lax.rem(slab, 2)
     me = side * heads + lax.axis_index("head")
     clip = lax.axis_index("dp")
 
     def ring_id(p):
-        return {"slab": 2 * plane + p // heads, "head": p % heads}
+        return {"slab": 2 * plane + lax.div(p, heads), "head": lax.rem(p, heads)}
 
     def plane_id(z):
         return {"slab": 2 * z + side}
@@ -58,7 +58,8 @@
         return pl.ds(pl.multiple_of(p * HD, HD), HD)
 
     def peer(s):
-        off = jnp.where(s % 2 == 1, (s + 1) // 2, ring - s // 2)
+        half = lax.div(s + 1, 2)
+        off = jnp.where(lax.rem(s, 2) == 1, half, ring - half)
         return lax.rem(me + off, ring)
 
     below = lax.rem(plane + planes - 1, planes)
@@ -94,7 +95,7 @@
     lax.fori_loop(1, clips, greet_clip, 0)
     pl.semaphore_wait(barrier, ring - 1 + planes - 1 + clips - 1)
 
-    arrays = ((k_in, kraw, TILE), (v_in, vbuf, TILE), (q_in, qraw, 0), (d_in, dbuf, 0))
+    arrays = ((k_in, kraw, TILE), (q_in, qraw, 0), (v_in, vbuf, TILE), (d_in, dbuf, 0))
     for i, (src, dst, base) in enumerate(arrays):
         pltpu.make_async_copy(
             src.at[0, :, cols(me)], dst.at[rows(me, base), :], in_recv.at[i, side]
@@ -136,17 +137,19 @@
             device_id_type=MESH,
         )
 
-    kv_copies = []
-    for i, buf in ((0, kraw), (1, vbuf)):
+    kv_copies = {}
+
+    def forward_kv(i, buf, arr):
         for up in (0, 1):
-            wait_bytes(buf.at[tile(1 + up), :], in_recv.at[i, up])
-            copy = kv_copy(i, buf, up)
-            copy.start()
-            kv_copies.append(copy)
-        send_in(2 + i)
-
+            wait_bytes(buf.at[tile(1 + up), :], in_recv.at[arr, up])
+            kv_copies[i, up] = kv_copy(i, buf, up)
+            kv_copies[i, up].start()
+
+    forward_kv(0, kraw, 0)
+    send_in(2)
     for copy in small:
         copy.wait()
+
     g0 = gains[0:1, :]
     g1 = gains[1:2, :]
 
@@ -160,8 +163,8 @@
         n = unit * g1
         knorm[tile(t), :] = n.astype(BF16)
         knt[:, tile(t)] = n.T.astype(BF16)
+        kunit[tile(t), :] = unit
         if t in (1, 2):
-            kunit[tile(t - 1), :] = unit
             krb[tile(t - 1), :] = jnp.broadcast_to(r, unit.shape)
 
     def do_v(t):
@@ -169,34 +172,45 @@
 
     do_k(1)
     do_k(2)
-    do_v(1)
-    do_v(2)
-    for t, up in ((0, 1), (3, 0)):
-        kv_copies[up].wait_recv()
-        do_k(t)
-        kv_copies[2 + up].wait_recv()
-        do_v(t)
-
-    invs = []
-    outs = []
     for a in (0, 1):
-        wait_bytes(qraw.at[tile(a), :], in_recv.at[2, a])
+        wait_bytes(qraw.at[tile(a), :], in_recv.at[1, a])
         unit, r = norm(qraw[tile(a), :])
         qunit[tile(a), :] = unit
         qrb[tile(a), :] = jnp.broadcast_to(r, unit.shape)
         qs[tile(a), :] = (unit * (g0 * (SCALE * LOG2E))).astype(BF16)
+    send_in(3)
+
+    dens = [jnp.zeros((1, TILE), F32), jnp.zeros((1, TILE), F32)]
+
+    def score(a, j):
+        on = mask[j, 0, 2 * plane + a].astype(F32)
+        s = dot(knorm[tile(a + j), :], qs[tile(a), :], ((1,), (1,)))
+        e = jnp.exp2(s) * on
+        dens[a] = dens[a] + jnp.sum(e, axis=0, keepdims=True)
+        expo[a, tile(j), :] = e.astype(BF16)
+
+    score(0, 1)
+    score(0, 2)
+    score(1, 0)
+    score(1, 1)
+    kv_copies[0, 1].wait_recv()
+    do_k(0)
+    score(0, 0)
+    kv_copies[0, 0].wait_recv()
+    do_k(3)
+    score(1, 2)
+    forward_kv(1, vbuf, 2)
+    do_v(1)
+    do_v(2)
+    invs = [1.0 / dens[0], 1.0 / dens[1]]
+    kv_copies[1, 1].wait_recv()
+    do_v(0)
+    kv_copies[1, 0].wait_recv()
+    do_v(3)
+    outs = []
     for a in (0, 1):
-        den = jnp.zeros((1, TILE), F32)
-        for j in range(3):
-            on = mask[j, 0, 2 * plane + a].astype(F32)
-            s = dot(knorm[tile(a + j), :], qs[tile(a), :], ((1,), (1,)))
-            e = jnp.exp2(s) * on
-            den = den + jnp.sum(e, axis=0, keepdims=True)
-            expo[a, tile(j), :] = e.astype(BF16)
-        inv = 1.0 / den
-        out_t = (dot(vt[:, a * TILE : (a + 3) * TILE], expo[a]) * inv).astype(BF16).astype(F32)
+        out_t = (dot(vt[:, a * TILE : (a + 3) * TILE], expo[a]) * invs[a]).astype(BF16).astype(F32)
         att[tile(a), :] = out_t.T.astype(BF16)
-        invs.append(inv)
         outs.append(out_t)
 
     def send_out(i, buf, out, a):
@@ -244,6 +258,13 @@
         dp = dot(vbuf[tile(a + j), :], douts[a])
         dsc[a, tile(j), :] = (expo[a, tile(j), :].astype(F32) * (dp - deltas[a])).astype(BF16)
 
+    def norm_backward(unit, r, gain, grad):
+        inner = grad * gain
+        return r * (inner - unit * jnp.mean(inner * unit, axis=-1, keepdims=True))
+
+    gain_q = jnp.zeros((1, HD), F32)
+    gain_k = jnp.zeros((1, HD), F32)
+    dqs = []
     for a in (0, 1):
         wait_bytes(dbuf.at[tile(a), :], in_recv.at[3, a])
         dt = dbuf[tile(a), :].astype(F32).T * invs[a]
@@ -256,33 +277,22 @@
         halo_copies[1, a] = halo_copy(1, a)
         halo_copies[1, a].start()
         dscore(a, j)
-        halo_out[0, a] = (dot(dsc[a, tile(j), :], qs[tile(a), :]) * LN2).astype(BF16)
+        dk = dot(dsc[a, tile(j), :], qs[tile(a), :]) * LN2
+        halo_out[0, a] = dk.astype(BF16)
         halo_copies[0, a] = halo_copy(0, a)
         halo_copies[0, a].start()
-
-    def norm_backward(unit, r, gain, grad):
-        inner = grad * gain
-        return r * (inner - unit * jnp.mean(inner * unit, axis=-1, keepdims=True))
-
-    gain_q = jnp.zeros((1, HD), F32)
-    for a in (0, 1):
-        for j in range(3):
-            if j != 2 * a:
-                dscore(a, j)
+        gain_k = gain_k + jnp.sum(dk * kunit[tile(3 * a), :], axis=0, keepdims=True)
+        dscore(a, 1)
+        dscore(a, 2 - j)
         dq = dot(knt[:, a * TILE : (a + 3) * TILE], dsc[a]).T * SCALE
-        unit = qunit[tile(a), :]
-        gain_q = gain_q + jnp.sum(dq * unit, axis=0, keepdims=True)
-        qg[tile(a), :] = norm_backward(unit, qrb[tile(a), :], g0, dq).astype(BF16)
-        send_out(1, qg, qg_out, a)
-
-    gain_k = jnp.zeros((1, HD), F32)
+        gain_q = gain_q + jnp.sum(dq * qunit[tile(a), :], axis=0, keepdims=True)
+        dqs.append(dq)
+    dks = []
     for t in (0, 1):
         dk = dot(dsc[0, tile(1 + t), :], qs[tile(0), :]) + dot(dsc[1, tile(t), :], qs[tile(1), :])
-        halo_copies[0, 1 - t].wait_recv()
-        dk = dk * LN2 + halo_in[0, 1 - t].astype(F32)
-        unit = kunit[tile(t), :]
-        gain_k = gain_k + jnp.sum(dk * unit, axis=0, keepdims=True)
-        kg[tile(t), :] = norm_backward(unit, krb[tile(t), :], g1, dk).astype(BF16)
+        dk = dk * LN2
+        gain_k = gain_k + jnp.sum(dk * kunit[tile(1 + t), :], axis=0, keepdims=True)
+        dks.append(dk)
 
     stages = (
         (gring, me, ring, ring_id),
@@ -314,22 +324,28 @@
         return jnp.sum(buf[...], axis=0)
 
     gain_start(0, jnp.concatenate([gain_q, gain_k, jnp.zeros((6, HD), F32)], axis=0))
+    for a in (0, 1):
+        qg[tile(a), :] = norm_backward(qunit[tile(a), :], qrb[tile(a), :], g0, dqs[a]).astype(BF16)
+        send_out(1, qg, qg_out, a)
     for t in (0, 1):
         dv = dot(expo[0, tile(1 + t), :], doscs[0]) + dot(expo[1, tile(t), :], doscs[1])
         halo_copies[1, 1 - t].wait_recv()
         vg[tile(t), :] = (dv + halo_in[1, 1 - t].astype(F32)).astype(BF16)
+        halo_copies[0, 1 - t].wait_recv()
+        dk = dks[t] + halo_in[0, 1 - t].astype(F32)
+        kg[tile(t), :] = norm_backward(kunit[tile(1 + t), :], krb[tile(t), :], g1, dk).astype(BF16)
+    gain_start(1, gain_end(0))
+    for t in (0, 1):
         send_out(3, vg, vg_out, t)
-    gain_start(1, gain_end(0))
-    send_out(2, kg, kg_out, 0)
+        send_out(2, kg, kg_out, t)
     gain_start(2, gain_end(1))
-    send_out(2, kg, kg_out, 1)
     gain_out[...] = gain_end(2)[0:2, :] * (1.0 / math.sqrt(total))
 
     for i in range(4):
         wait_bytes(att.at[pl.ds(0, 2 * TILE), :], out_recv.at[i])
         wait_bytes(att.at[pl.ds(0, 2 * TILE - chunk), :], out_send.at[i])
         wait_bytes(att.at[pl.ds(0, 2 * TILE - chunk), :], in_send.at[i])
-    for copy in kv_copies:
+    for copy in kv_copies.values():
         copy.wait_send()
     for copy in halo_copies.values():
         copy.wait_send()
@@ -377,7 +393,7 @@
                 pltpu.VMEM((HD, 4 * TILE), BF16),
                 pltpu.VMEM((HD, 4 * TILE), BF16),
                 pltpu.VMEM((2 * TILE, HD), BF16),
-                pltpu.VMEM((2 * TILE, HD), F32),
+                pltpu.VMEM((4 * TILE, HD), F32),
                 pltpu.VMEM((2 * TILE, HD), F32),
                 pltpu.VMEM((2 * TILE, HD), F32),
                 pltpu.VMEM((2 * TILE, HD), F32),
@@ -416,7 +432,8 @@
             in_specs=[vmem] * 5,
             out_specs=(hbm,) * 5,
             scratch_shapes=[dma((5,))],
-        )(*outs)
+            compiler_params=pltpu.CompilerParams(vmem_limit_bytes=4 * 1024 * 1024),
+        )(*(pltpu.with_memory_space_constraint(x, pltpu.VMEM) for x in outs))
 
     tokens = P("dp", ("slab", "head"), None)
     return jax.shard_map(

time: 65 us -> 58.8 us (0.905)
  local copies, waits for them, and re-layouts: 3.26 us -> 0 us
  Pallas kernels: 60.5 us -> 58 us
    unnamed x10 -> x0, local copies, waits for them, and re-layouts: 3.26 us -> none
    pallas_call x1, Pallas kernels: 58.3 us -> 57.1 us  [local(): pl.pallas_call(functools.partial(kernel, sizes), out_shape=landing, in_sp...]
    pallas_call x1, Pallas kernels: 2.13 us -> 0.92 us  [local(): pl.pallas_call(store, out_shape=outs_shape, in_specs=[vmem] * 5, out_spec...]
where the time goes in v4:
time: 58.8 us; the launch traced here: 58.7 us
  Pallas kernels  58 us (99%)
  between operations  0.64 us (1%)
    pallas_call x1, Pallas kernels, local(): pl.pallas_call(functools.partial(kernel, sizes), out_shape=landing, in_sp...  57.1 us

profile of v4, /device:TPU:1, one launch (start us, length us, event | category | flops | bytes accessed | tf_op | source)
XLA Modules:
  0.0 58.7 jit_solution(7057348271794391841)
XLA Ops:
  0.6 57.1 %shard_map.101 = (bf16[1,48,2048]{2,1,0:T(8,128)(2,1)S(1)}, bf16[1,48,2048]{2,1,0:T(8,128)(2,1)S(1)}, bf16[1,48,2048]{2,1,0:T(8,128)(2,1)S(1)}, bf16[1,48,2048]{2,1,0:T(8,128)(2,1)S(1)}, f32[2,128]{1,0:T(2,128)S(1)}) custom-call(bf16[1,48,2048]{2,1,0:T(8,128)(2,1)} %q_in.1, bf16[1,48,2048]{2,1,0:T(8,128)(2,1)} %k_in.1, bf16[1,48,2048]{2,1,0:T(8,128)(2,1)} %v_in.1, ...), custom_call_target="tpu_custom_call" | custom-call | tf_op jit(solution)/shard_map/pallas_call | solution.py:382
  57.7 0.9 %shard_map.102 = (bf16[1,48,2048]{2,1,0:T(8,128)(2,1)}, bf16[1,48,2048]{2,1,0:T(8,128)(2,1)}, bf16[1,48,2048]{2,1,0:T(8,128)(2,1)}, bf16[1,48,2048]{2,1,0:T(8,128)(2,1)}, f32[2,128]{1,0:T(2,128)}) custom-call(bf16[1,48,2048]{2,1,0:T(8,128)(2,1)S(1)} %get-tuple-element.10.refs_0_, bf16[1,48,2048]{2,1,0:T(8,128)(2,1)S(1)} %get-tuple-element.11.refs_1_, ...), custom_call_target="tpu_custom_call" | custom-call | tf_op jit(solution)/shard_map/pallas_call | solution.py:429

commit v5 on v4

--- a/solution.py
+++ b/solution.py
@@ -57,10 +57,10 @@
     def cols(p):
         return pl.ds(pl.multiple_of(p * HD, HD), HD)
 
+    stride = 7 + 2 * lax.rem(me, 2)
+
     def peer(s):
-        half = lax.div(s + 1, 2)
-        off = jnp.where(lax.rem(s, 2) == 1, half, ring - half)
-        return lax.rem(me + off, ring)
+        return lax.rem(me + s * stride, ring)
 
     below = lax.rem(plane + planes - 1, planes)
     above = lax.rem(plane + 1, planes)
@@ -95,13 +95,13 @@
     lax.fori_loop(1, clips, greet_clip, 0)
     pl.semaphore_wait(barrier, ring - 1 + planes - 1 + clips - 1)
 
-    arrays = ((k_in, kraw, TILE), (q_in, qraw, 0), (v_in, vbuf, TILE), (d_in, dbuf, 0))
+    arrays = ((k_in, kraw, TILE), (v_in, vbuf, TILE), (q_in, qraw, 0), (d_in, dbuf, 0))
     for i, (src, dst, base) in enumerate(arrays):
         pltpu.make_async_copy(
             src.at[0, :, cols(me)], dst.at[rows(me, base), :], in_recv.at[i, side]
         ).start()
 
-    def send_in(i):
+    def send_in(i, first=1, end=ring):
         src, dst, base = arrays[i]
 
         def step(s, c):
@@ -116,7 +116,7 @@
             ).start()
             return c
 
-        lax.fori_loop(1, ring, step, 0)
+        lax.fori_loop(first, end, step, 0)
 
     send_in(0)
     send_in(1)
@@ -146,7 +146,10 @@
             kv_copies[i, up].start()
 
     forward_kv(0, kraw, 0)
-    send_in(2)
+    send_in(2, 1, heads)
+    forward_kv(1, vbuf, 1)
+    send_in(2, heads, ring)
+    send_in(3)
     for copy in small:
         copy.wait()
 
@@ -172,13 +175,20 @@
 
     do_k(1)
     do_k(2)
+    do_v(1)
+    do_v(2)
+    for t, up in ((0, 1), (3, 0)):
+        kv_copies[0, up].wait_recv()
+        do_k(t)
+    for t, up in ((0, 1), (3, 0)):
+        kv_copies[1, up].wait_recv()
+        do_v(t)
     for a in (0, 1):
-        wait_bytes(qraw.at[tile(a), :], in_recv.at[1, a])
+        wait_bytes(qraw.at[tile(a), :], in_recv.at[2, a])
         unit, r = norm(qraw[tile(a), :])
         qunit[tile(a), :] = unit
         qrb[tile(a), :] = jnp.broadcast_to(r, unit.shape)
         qs[tile(a), :] = (unit * (g0 * (SCALE * LOG2E))).astype(BF16)
-    send_in(3)
 
     dens = [jnp.zeros((1, TILE), F32), jnp.zeros((1, TILE), F32)]
 
@@ -189,55 +199,33 @@
         dens[a] = dens[a] + jnp.sum(e, axis=0, keepdims=True)
         expo[a, tile(j), :] = e.astype(BF16)
 
-    score(0, 1)
-    score(0, 2)
-    score(1, 0)
-    score(1, 1)
-    kv_copies[0, 1].wait_recv()
-    do_k(0)
-    score(0, 0)
-    kv_copies[0, 0].wait_recv()
-    do_k(3)
-    score(1, 2)
-    forward_kv(1, vbuf, 2)
-    do_v(1)
-    do_v(2)
-    invs = [1.0 / dens[0], 1.0 / dens[1]]
-    kv_copies[1, 1].wait_recv()
-    do_v(0)
-    kv_copies[1, 0].wait_recv()
-    do_v(3)
+    def send_out(i, buf, out, first=1, end=ring):
+        def step(s, c):
+            p = peer(s)
+            pltpu.make_async_remote_copy(
+                src_ref=buf.at[rows(p), :],
+                dst_ref=out.at[0, :, cols(me)],
+                send_sem=out_send.at[i],
+                recv_sem=out_recv.at[i],
+                device_id=ring_id(p),
+                device_id_type=MESH,
+            ).start()
+            return c
+
+        if first == 1:
+            pltpu.make_async_copy(buf.at[rows(me), :], out.at[0, :, cols(me)], out_recv.at[i]).start()
+        lax.fori_loop(first, end, step, 0)
+
+    invs = []
     outs = []
     for a in (0, 1):
+        for j in range(3):
+            score(a, j)
+        invs.append(1.0 / dens[a])
         out_t = (dot(vt[:, a * TILE : (a + 3) * TILE], expo[a]) * invs[a]).astype(BF16).astype(F32)
         att[tile(a), :] = out_t.T.astype(BF16)
         outs.append(out_t)
-
-    def send_out(i, buf, out, a):
-        def step(s, c):
-            p = a * heads + lax.rem(me + s, heads)
-
-            @pl.when(p != me)
-            def _():
-                pltpu.make_async_remote_copy(
-                    src_ref=buf.at[rows(p), :],
-                    dst_ref=out.at[0, :, cols(me)],
-                    send_sem=out_send.at[i],
-                    recv_sem=out_recv.at[i],
-                    device_id=ring_id(p),
-                    device_id_type=MESH,
-                ).start()
-
-            @pl.when(p == me)
-            def _():
-                pltpu.make_async_copy(buf.at[rows(p), :], out.at[0, :, cols(p)], out_recv.at[i]).start()
-
-            return c
-
-        lax.fori_loop(0, heads, step, 0)
-
-    send_out(0, att, att_out, 0)
-    send_out(0, att, att_out, 1)
+    send_out(0, att, att_out)
 
     def halo_copy(i, up):
         return pltpu.make_async_remote_copy(
@@ -326,19 +314,20 @@
     gain_start(0, jnp.concatenate([gain_q, gain_k, jnp.zeros((6, HD), F32)], axis=0))
     for a in (0, 1):
         qg[tile(a), :] = norm_backward(qunit[tile(a), :], qrb[tile(a), :], g0, dqs[a]).astype(BF16)
-        send_out(1, qg, qg_out, a)
+    send_out(1, qg, qg_out)
     for t in (0, 1):
         dv = dot(expo[0, tile(1 + t), :], doscs[0]) + dot(expo[1, tile(t), :], doscs[1])
         halo_copies[1, 1 - t].wait_recv()
         vg[tile(t), :] = (dv + halo_in[1, 1 - t].astype(F32)).astype(BF16)
+    send_out(3, vg, vg_out)
+    gain_start(1, gain_end(0))
+    for t in (0, 1):
         halo_copies[0, 1 - t].wait_recv()
         dk = dks[t] + halo_in[0, 1 - t].astype(F32)
         kg[tile(t), :] = norm_backward(kunit[tile(1 + t), :], krb[tile(t), :], g1, dk).astype(BF16)
-    gain_start(1, gain_end(0))
-    for t in (0, 1):
-        send_out(3, vg, vg_out, t)
-        send_out(2, kg, kg_out, t)
+    send_out(2, kg, kg_out, 1, heads)
     gain_start(2, gain_end(1))
+    send_out(2, kg, kg_out, heads, ring)
     gain_out[...] = gain_end(2)[0:2, :] * (1.0 / math.sqrt(total))
 
     for i in range(4):

time: 58.8 us -> 58.2 us (0.990)
  Pallas kernels: 58 us -> 57.4 us
    pallas_call x1, Pallas kernels: 57.1 us -> 56.5 us  [local(): pl.pallas_call(functools.partial(kernel, sizes), out_shape=landing, in_sp...]
where the time goes in v5:
time: 58.2 us; the launch traced here: 58.1 us
  Pallas kernels  57.4 us (99%)
  between operations  0.64 us (1%)
    pallas_call x1, Pallas kernels, local(): pl.pallas_call(functools.partial(kernel, sizes), out_shape=landing, in_sp...  56.5 us

profile of v5, /device:TPU:1, one launch (start us, length us, event | category | flops | bytes accessed | tf_op | source)
XLA Modules:
  0.0 58.1 jit_solution(6517950914815403019)
XLA Ops:
  0.6 56.5 %shard_map.101 = (bf16[1,48,2048]{2,1,0:T(8,128)(2,1)S(1)}, bf16[1,48,2048]{2,1,0:T(8,128)(2,1)S(1)}, bf16[1,48,2048]{2,1,0:T(8,128)(2,1)S(1)}, bf16[1,48,2048]{2,1,0:T(8,128)(2,1)S(1)}, f32[2,128]{1,0:T(2,128)S(1)}) custom-call(bf16[1,48,2048]{2,1,0:T(8,128)(2,1)} %q_in.1, bf16[1,48,2048]{2,1,0:T(8,128)(2,1)} %k_in.1, bf16[1,48,2048]{2,1,0:T(8,128)(2,1)} %v_in.1, ...), custom_call_target="tpu_custom_call" | custom-call | tf_op jit(solution)/shard_map/pallas_call | solution.py:371
  57.1 0.9 %shard_map.102 = (bf16[1,48,2048]{2,1,0:T(8,128)(2,1)}, bf16[1,48,2048]{2,1,0:T(8,128)(2,1)}, bf16[1,48,2048]{2,1,0:T(8,128)(2,1)}, bf16[1,48,2048]{2,1,0:T(8,128)(2,1)}, f32[2,128]{1,0:T(2,128)}) custom-call(bf16[1,48,2048]{2,1,0:T(8,128)(2,1)S(1)} %get-tuple-element.10.refs_0_, bf16[1,48,2048]{2,1,0:T(8,128)(2,1)S(1)} %get-tuple-element.11.refs_1_, ...), custom_call_target="tpu_custom_call" | custom-call | tf_op jit(solution)/shard_map/pallas_call | solution.py:418

commit v6 on v5

v6 whole, which is shorter than its diff:
```python
import functools
import math

import jax
import jax.numpy as jnp
from jax import lax
from jax.experimental import pallas as pl
from jax.experimental.pallas import tpu as pltpu
from jax.sharding import PartitionSpec as P

MESH = pl.DeviceIdType.MESH
TILE = 384
HD = 128
EPS = 1e-06
SCALE = HD**-0.5
LOG2E = math.log2(math.e)
LN2 = math.log(2.0)
F32 = jnp.float32
BF16 = jnp.bfloat16


def dot(a, b, dims=((1,), (0,))):
    return lax.dot_general(a, b, (dims, ((), ())), preferred_element_type=F32)


def kernel(
    sizes,
    q_in, k_in, v_in, d_in, gains_in, mask_in,
    land, gain_out,
    rx, kh, vh,
    knorm, knt, vt, qs, qst,
    kunit, krb, qunit, qrb,
    expo, dsc, ob, hg_out, hg_in,
    gring, gz, gx, gains, mask,
    small_sem, in_send, in_recv, kv_send, kv_recv, hg_send, hg_recv, out_send, out_recv, g_send, g_recv,
):
    heads, planes, clips, total = sizes
    ring = 2 * heads
    chips = heads
    chunk = TILE // heads
    pair = 2 * HD
    slab = lax.axis_index("slab")
    head = lax.axis_index("head")
    clip = lax.axis_index("dp")
    plane = lax.div(slab, 2)
    side = lax.rem(slab, 2)
    core = lax.rem(head, 2)
    me = side * heads + head
    chip = lax.div(me, 2)
    tile = 2 * plane + core

    def ring_id(p):
        return {"slab": 2 * plane + lax.div(p, heads), "head": lax.rem(p, heads)}

    def plane_id(z):
        return {"slab": 2 * z + side}

    def rows(n):
        return pl.ds(pl.multiple_of(n * chunk, 16), chunk)

    def cols(c):
        return pl.ds(pl.multiple_of(c * pair, pair), pair)

    stride = 3 + 2 * core

    other = head + 1 - 2 * core
    next_plane = lax.rem(plane + planes - 1 + 2 * core, planes)
    near = ({"head": other}, {"slab": 2 * next_plane + side, "head": other})
    slots = (1, 2 - 2 * core, 2 * core)

    small = [
        pltpu.make_async_copy(gains_in, gains, small_sem.at[0]),
        pltpu.make_async_copy(mask_in, mask, small_sem.at[1]),
    ]
    for copy in small:
        copy.start()

    barrier = pltpu.get_barrier_semaphore()

    def greet(target):
        pl.semaphore_signal(barrier, inc=1, device_id=target, device_id_type=MESH)

    def greet_ring(s, c):
        greet(ring_id(lax.rem(me + s, ring)))
        return c

    def greet_plane(s, c):
        greet(plane_id(lax.rem(plane + s, planes)))
        return c

    def greet_clip(s, c):
        greet({"dp": lax.rem(clip + s, clips)})
        return c

    lax.fori_loop(1, ring, greet_ring, 0)
    greet(near[1])
    lax.fori_loop(1, planes, greet_plane, 0)
    lax.fori_loop(1, clips, greet_clip, 0)
    pl.semaphore_wait(barrier, ring + planes - 1 + clips - 1)

    def wait_bytes(ref, sem):
        pltpu.make_async_copy(ref, ref, sem).wait()

    def remote(src, dst, send_sem, recv_sem, target):
        return pltpu.make_async_remote_copy(
            src_ref=src,
            dst_ref=dst,
            send_sem=send_sem,
            recv_sem=recv_sem,
            device_id=target,
            device_id_type=MESH,
        )

    sources = (k_in, v_in, q_in, d_in)

    def send_in(i, first=1, end=chips):
        def block(c):
            return sources[i].at[0, :, cols(c)], rx.at[i, rows(head), :]

        def to(c):
            src, dst = block(c)
            remote(src, dst, in_send.at[i], in_recv.at[i], ring_id(2 * c + side)).start()

        def step(s, carry):
            to(lax.rem(chip + s * stride, chips))
            return carry

        lax.fori_loop(first, end, step, 0)
        if end == chips:

            @pl.when(core != side)
            def _():
                to(chip)

            @pl.when(core == side)
            def _():
                src, dst = block(chip)
                pltpu.make_async_copy(src, dst, in_recv.at[i]).start()

    def wait_in(i):
        wait_bytes(rx.at[i], in_recv.at[i])

    def near_copies(src, dst, send_sem, recv_sem, which=(1, 0)):
        copies = [None, None]
        for n in which:
            copies[n] = remote(src(n), dst(n), send_sem.at[n], recv_sem.at[n], near[n])
            copies[n].start()
        return copies

    send_in(0)
    send_in(1)
    wait_in(0)
    k_copies = near_copies(lambda n: rx.at[0], lambda n: kh.at[n], kv_send.at[0], kv_recv.at[0])
    send_in(2, 1, chips // 2)
    wait_in(1)
    v_copies = near_copies(lambda n: rx.at[1], lambda n: vh.at[n], kv_send.at[1], kv_recv.at[1])
    send_in(2, chips // 2, chips)
    send_in(3)
    for copy in small:
        copy.wait()

    g0 = gains[0:1, :]
    g1 = gains[1:2, :]
    both = tuple((h, slice(h * HD, (h + 1) * HD)) for h in (0, 1))

    def norm(raw):
        x = raw.astype(F32)
        r = lax.rsqrt(jnp.mean(x * x, axis=-1, keepdims=True) + EPS)
        return x * r, r

    def span(slot):
        return slice(slot * TILE, (slot + 1) * TILE)

    def keys(slot):
        return rx.at[0] if slot == 0 else kh.at[slot - 1]

    def vals(slot):
        return rx.at[1] if slot == 0 else vh.at[slot - 1]

    def do_k(slot):
        for h, at in both:
            unit, r = norm(keys(slot)[:, at])
            n = (unit * g1).astype(BF16)
            knorm[h, span(slot), :] = n
            knt[h, :, span(slot)] = n.T
            kunit[h, span(slot), :] = unit
            if slot == 0:
                krb[h] = jnp.broadcast_to(r, unit.shape)

    def do_v(slot):
        for h, at in both:
            vt[h, :, span(slot)] = vals(slot)[:, at].T

    dens = [jnp.zeros((1, TILE), F32), jnp.zeros((1, TILE), F32)]

    def score(slot):
        on = mask[slots[slot], 0, tile].astype(F32)
        for h, _ in both:
            e = jnp.exp2(dot(knorm[h, span(slot), :], qst[h])) * on
            dens[h] = dens[h] + jnp.sum(e, axis=0, keepdims=True)
            expo[h, span(slot), :] = e.astype(BF16)

    do_k(0)
    do_v(0)
    k_copies[0].wait_recv()
    do_k(1)
    k_copies[1].wait_recv()
    do_k(2)
    v_copies[0].wait_recv()
    do_v(1)
    v_copies[1].wait_recv()
    do_v(2)
    wait_in(2)
    for h, at in both:
        unit, r = norm(rx[2, :, at])
        qunit[h] = unit
        qrb[h] = jnp.broadcast_to(r, unit.shape)
        n = (unit * (g0 * (SCALE * LOG2E))).astype(BF16)
        qs[h] = n
        qst[h] = n.T
    for slot in range(3):
        score(slot)
    invs = [1.0 / dens[0], 1.0 / dens[1]]

    def send_out(i, first=1, end=heads):
        def block(n):
            return ob.at[i, rows(n), :], land.at[i, :, cols(chip)]

        def to(n):
            src, dst = block(n)
            remote(src, dst, out_send.at[i], out_recv.at[i], {"slab": tile, "head": n}).start()

        def step(s, carry):
            to(lax.rem(head + s * stride, heads))
            return carry

        lax.fori_loop(first, end, step, 0)
        if end == heads:

            @pl.when(core != side)
            def _():
                to(head)

            @pl.when(core == side)
            def _():
                src, dst = block(head)
                pltpu.make_async_copy(src, dst, out_recv.at[i]).start()

    outs = []
    for h, at in both:
        out_t = (dot(vt[h], expo[h]) * invs[h]).astype(BF16)
        ob[0, :, at] = out_t.T
        outs.append(out_t.astype(F32))
    send_out(0)

    def norm_backward(unit, r, gain, grad):
        inner = grad * gain
        return r * (inner - unit * jnp.mean(inner * unit, axis=-1, keepdims=True))

    douts = []
    doscs = []
    deltas = []

    def dscore(slot):
        for h, at in both:
            dp = dot(vals(slot)[:, at], douts[h])
            dsc[h, span(slot), :] = (expo[h, span(slot), :].astype(F32) * (dp - deltas[h])).astype(BF16)

    wait_in(3)
    for h, at in both:
        dt = rx[3, :, at].T.astype(F32) * invs[h]
        dtb = dt.astype(BF16)
        douts.append(dtb)
        deltas.append(jnp.sum(dtb.astype(F32) * outs[h], axis=0, keepdims=True))

    hg_copies = {}

    def send_near(i, n):
        hg_copies[i, n] = remote(hg_out.at[i, n], hg_in.at[i, n], hg_send.at[i, n], hg_recv.at[i, n], near[n])
        hg_copies[i, n].start()

    gain_k = jnp.zeros((1, HD), F32)
    dks = []
    for slot in (2, 1, 0):
        dscore(slot)
        for h, at in both:
            dk = dot(dsc[h, span(slot), :], qs[h]) * LN2
            gain_k = gain_k + jnp.sum(dk * kunit[h, span(slot), :], axis=0, keepdims=True)
            if slot > 0:
                hg_out[0, slot - 1, :, at] = dk.astype(BF16)
            else:
                dks.append(dk)
        if slot > 0:
            send_near(0, slot - 1)
    gain_q = jnp.zeros((1, HD), F32)
    dqs = []
    for h, at in both:
        dq = dot(knt[h], dsc[h]).T * SCALE
        gain_q = gain_q + jnp.sum(dq * qunit[h], axis=0, keepdims=True)
        dqs.append(dq)

    stages = (
        (gring, me, ring, ring_id),
        (gz, plane, planes, plane_id),
        (gx, clip, clips, lambda x: {"dp": x}),
    )

    def gain_start(which, part):
        buf, here, count, target = stages[which]
        buf[here] = part

        def step(s, c):
            remote(
                buf.at[here], buf.at[here], g_send.at[which], g_recv.at[which], target(lax.rem(here + s, count))
            ).start()
            return c

        lax.fori_loop(1, count, step, 0)

    def gain_end(which):
        buf, _, count, _ = stages[which]
        if count > 1:
            wait_bytes(buf.at[pl.ds(0, count - 1)], g_recv.at[which])
        return jnp.sum(buf[...], axis=0)

    gain_start(0, jnp.concatenate([gain_q, gain_k, jnp.zeros((6, HD), F32)], axis=0))
    for h, at in both:
        doscs.append(douts[h].T)
    for n in (1, 0):
        for h, at in both:
            hg_out[1, n, :, at] = dot(expo[h, span(n + 1), :], doscs[h]).astype(BF16)
        send_near(1, n)
    for h, at in both:
        ob[1, :, at] = norm_backward(qunit[h], qrb[h], g0, dqs[h]).astype(BF16)
    send_out(1)
    hg_copies[0, 0].wait_recv()
    hg_copies[0, 1].wait_recv()
    for h, at in both:
        dk = dks[h] + hg_in[0, 0, :, at].astype(F32) + hg_in[0, 1, :, at].astype(F32)
        ob[3, :, at] = norm_backward(kunit[h, span(0), :], krb[h], g1, dk).astype(BF16)
    gain_start(1, gain_end(0))
    send_out(3)
    hg_copies[1, 0].wait_recv()
    hg_copies[1, 1].wait_recv()
    for h, at in both:
        dv = dot(expo[h, span(0), :], doscs[h])
        ob[2, :, at] = (dv + hg_in[1, 0, :, at].astype(F32) + hg_in[1, 1, :, at].astype(F32)).astype(BF16)
    send_out(2, 1, heads // 2)
    gain_start(2, gain_end(1))
    send_out(2, heads // 2, heads)
    gain_out[...] = gain_end(2)[0:2, :] * (1.0 / math.sqrt(total))

    def wait_sent(count):
        for i in range(4):
            wait_bytes(rx.at[i, pl.ds(0, count * chunk), :], in_send.at[i])
            wait_bytes(ob.at[i, pl.ds(0, count * chunk), :], out_send.at[i])

    for i in range(4):
        wait_bytes(ob.at[i], out_recv.at[i])
    for copy in k_copies + v_copies + list(hg_copies.values()):
        copy.wait_send()
    for which, (buf, _, count, _) in enumerate(stages):
        if count > 1:
            wait_bytes(buf.at[pl.ds(0, count - 1)], g_send.at[which])

    @pl.when(core == side)
    def _():
        wait_sent(heads - 1)

    @pl.when(core != side)
    def _():
        wait_sent(heads)


def store(land, gain, att, qg, vg, kg, gain_out, sems):
    copies = [pltpu.make_async_copy(gain, gain_out, sems.at[4])]
    for i, out in enumerate((att, qg, vg, kg)):
        copies.append(pltpu.make_async_copy(land.at[i], out.at[0], sems.at[i]))
    for copy in copies:
        copy.start()
    for copy in copies:
        copy.wait()


def solution(mesh):
    heads = mesh.shape["head"]
    planes = mesh.shape["slab"] // 2
    clips = mesh.shape["dp"]
    ring = 2 * heads
    chunk = TILE // heads
    total = clips * planes * 2 * TILE * ring
    sizes = (heads, planes, clips, total)

    def local(q_proj, k_proj, v_proj, grad_out, norm_gains, window_mask):
        hbm = pl.BlockSpec(memory_space=pltpu.HBM)
        vmem = pl.BlockSpec(memory_space=pltpu.VMEM)
        big = jax.ShapeDtypeStruct(q_proj.shape, BF16)
        sums = jax.ShapeDtypeStruct((2, HD), F32)
        dma = pltpu.SemaphoreType.DMA
        wide = 2 * HD
        landing = (pltpu.VMEM((4, chunk, ring * HD), BF16), pltpu.VMEM((2, HD), F32))
        operands = (q_proj, k_proj, v_proj, grad_out, norm_gains, jnp.transpose(window_mask, (2, 0, 1)))
        outs = pl.pallas_call(
            functools.partial(kernel, sizes),
            out_shape=landing,
            in_specs=[hbm] * 6,
            out_specs=(vmem,) * 2,
            scratch_shapes=[
                pltpu.VMEM((4, TILE, wide), BF16),
                pltpu.VMEM((2, TILE, wide), BF16),
                pltpu.VMEM((2, TILE, wide), BF16),
                pltpu.VMEM((2, 3 * TILE, HD), BF16),
                pltpu.VMEM((2, HD, 3 * TILE), BF16),
                pltpu.VMEM((2, HD, 3 * TILE), BF16),
                pltpu.VMEM((2, TILE, HD), BF16),
                pltpu.VMEM((2, HD, TILE), BF16),
                pltpu.VMEM((2, 3 * TILE, HD), F32),
                pltpu.VMEM((2, TILE, HD), F32),
                pltpu.VMEM((2, TILE, HD), F32),
                pltpu.VMEM((2, TILE, HD), F32),
                pltpu.VMEM((2, 3 * TILE, TILE), BF16),
                pltpu.VMEM((2, 3 * TILE, TILE), BF16),
                pltpu.VMEM((4, TILE, wide), BF16),
                pltpu.VMEM((2, 2, TILE, wide), BF16),
                pltpu.VMEM((2, 2, TILE, wide), BF16),
                pltpu.VMEM((ring, 8, HD), F32),
                pltpu.VMEM((planes, 8, HD), F32),
                pltpu.VMEM((clips, 8, HD), F32),
                pltpu.VMEM((2, HD), F32),
                pltpu.SMEM((3, 1, 2 * planes), jnp.int32),
                dma((2,)),
                dma((4,)),
                dma((4,)),
                dma((2, 2)),
                dma((2, 2)),
                dma((2, 2)),
                dma((2, 2)),
                dma((4,)),
                dma((4,)),
                dma((3,)),
                dma((3,)),
            ],
            compiler_params=pltpu.CompilerParams(
                collective_id=0, has_side_effects=True, vmem_limit_bytes=40 * 1024 * 1024
            ),
        )(*(pltpu.with_memory_space_constraint(x, pltpu.HBM) for x in operands))
        att, qg, vg, kg, gain = pl.pallas_call(
            store,
            out_shape=(big, big, big, big, sums),
            in_specs=[vmem] * 2,
            out_specs=(hbm,) * 5,
            scratch_shapes=[dma((5,))],
            compiler_params=pltpu.CompilerParams(vmem_limit_bytes=4 * 1024 * 1024),
        )(*(pltpu.with_memory_space_constraint(x, pltpu.VMEM) for x in outs))
        return att, qg, kg, vg, gain

    tokens = P("dp", ("slab", "head"), None)
    return jax.shard_map(
        local,
        mesh=mesh,
        in_specs=(tokens, tokens, tokens, tokens, P(), P("dp", None, None)),
        out_specs=(tokens, tokens, tokens, tokens, P()),
        check_vma=False,
    )
```

time: 58.2 us -> 55.9 us (0.960)
  Pallas kernels: 57.4 us -> 55.1 us
    pallas_call x1, Pallas kernels: 56.5 us -> 54.2 us  [local(): pl.pallas_call(functools.partial(kernel, sizes), out_shape=landing, in_sp...]
where the time goes in v6:
time: 55.9 us; the launch traced here: 55.8 us
  Pallas kernels  55.1 us (99%)
  between operations  0.64 us (1%)
    pallas_call x1, Pallas kernels, local(): pl.pallas_call(functools.partial(kernel, sizes), out_shape=landing, in_sp...  54.2 us

profile of v6, /device:TPU:1, one launch (start us, length us, event | category | flops | bytes accessed | tf_op | source)
XLA Modules:
  0.0 55.8 jit_solution(7096047822427270992)
XLA Ops:
  0.6 54.2 %shard_map.101 = (bf16[4,48,2048]{2,1,0:T(8,128)(2,1)S(1)}, f32[2,128]{1,0:T(2,128)S(1)}) custom-call(bf16[1,48,2048]{2,1,0:T(8,128)(2,1)} %q_in.1, bf16[1,48,2048]{2,1,0:T(8,128)(2,1)} %k_in.1, bf16[1,48,2048]{2,1,0:T(8,128)(2,1)} %v_in.1, bf16[1,48,2048]{2,1,0:T(8,128)(2,1)} %d_in.1, f32[2,128]{1,0:T(2,128)} %gains_in.1, s32[3,1,16]{2,1,0:T(1,128)} %bitcast.1), custom_call_target="tpu_custom_call" | custom-call | tf_op jit(solution)/shard_map/pallas_call | solution.py:403
  54.9 0.9 %shard_map.102 = (bf16[1,48,2048]{2,1,0:T(8,128)(2,1)}, bf16[1,48,2048]{2,1,0:T(8,128)(2,1)}, bf16[1,48,2048]{2,1,0:T(8,128)(2,1)}, bf16[1,48,2048]{2,1,0:T(8,128)(2,1)}, f32[2,128]{1,0:T(2,128)}) custom-call(bf16[4,48,2048]{2,1,0:T(8,128)(2,1)S(1)} %get-tuple-element.12.land, f32[2,128]{1,0:T(2,128)S(1)} %get-tuple-element.13.gain), custom_call_target="tpu_custom_call" | custom-call | tf_op jit(solution)/shard_map/pallas_call | solution.py:447

commit v7 on v6

--- a/solution.py
+++ b/solution.py
@@ -224,7 +224,7 @@
 
     def send_out(i, first=1, end=heads):
         def block(n):
-            return ob.at[i, rows(n), :], land.at[i, :, cols(chip)]
+            return ob.at[i, rows(n), :], land.at[i, chip]
 
         def to(n):
             src, dst = block(n)
@@ -373,9 +373,15 @@
 
 
 def store(land, gain, att, qg, vg, kg, gain_out, sems):
-    copies = [pltpu.make_async_copy(gain, gain_out, sems.at[4])]
+    copies = [pltpu.make_async_copy(gain, gain_out, sems.at[4, 0])]
+    width = land.shape[3]
     for i, out in enumerate((att, qg, vg, kg)):
-        copies.append(pltpu.make_async_copy(land.at[i], out.at[0], sems.at[i]))
+        for c in range(land.shape[1]):
+            copies.append(
+                pltpu.make_async_copy(
+                    land.at[i, c], out.at[0, :, c * width : (c + 1) * width], sems.at[i, c]
+                )
+            )
     for copy in copies:
         copy.start()
     for copy in copies:
@@ -398,7 +404,7 @@
         sums = jax.ShapeDtypeStruct((2, HD), F32)
         dma = pltpu.SemaphoreType.DMA
         wide = 2 * HD
-        landing = (pltpu.VMEM((4, chunk, ring * HD), BF16), pltpu.VMEM((2, HD), F32))
+        landing = (pltpu.VMEM((4, heads, chunk, wide), BF16), pltpu.VMEM((2, HD), F32))
         operands = (q_proj, k_proj, v_proj, grad_out, norm_gains, jnp.transpose(window_mask, (2, 0, 1)))
         outs = pl.pallas_call(
             functools.partial(kernel, sizes),
@@ -449,7 +455,7 @@
             out_shape=(big, big, big, big, sums),
             in_specs=[vmem] * 2,
             out_specs=(hbm,) * 5,
-            scratch_shapes=[dma((5,))],
+            scratch_shapes=[dma((5, heads))],
             compiler_params=pltpu.CompilerParams(vmem_limit_bytes=4 * 1024 * 1024),
         )(*(pltpu.with_memory_space_constraint(x, pltpu.VMEM) for x in outs))
         return att, qg, kg, vg, gain

time: 55.9 us -> 56.2 us (level)
  no operation moved by 1% of the time
where the time goes in v7:
time: 56.2 us; the launch traced here: 56.1 us
  Pallas kernels  55.4 us (99%)
  between operations  0.64 us (1%)
    pallas_call x1, Pallas kernels, local(): pl.pallas_call(functools.partial(kernel, sizes), out_shape=landing, in_sp...  54.2 us
    pallas_call x1, Pallas kernels, local(): pl.pallas_call(store, out_shape=(big, big, big, big, sums), in_specs=[vme...  1.22 us

profile of v7, /device:TPU:1, one launch (start us, length us, event | category | flops | bytes accessed | tf_op | source)
XLA Modules:
  0.0 56.1 jit_solution(3604112816915755772)
XLA Ops:
  0.6 54.2 %shard_map.101 = (bf16[4,8,48,256]{3,2,1,0:T(8,128)(2,1)S(1)}, f32[2,128]{1,0:T(2,128)S(1)}) custom-call(bf16[1,48,2048]{2,1,0:T(8,128)(2,1)} %q_in.1, bf16[1,48,2048]{2,1,0:T(8,128)(2,1)} %k_in.1, bf16[1,48,2048]{2,1,0:T(8,128)(2,1)} %v_in.1, bf16[1,48,2048]{2,1,0:T(8,128)(2,1)} %d_in.1, f32[2,128]{1,0:T(2,128)} %gains_in.1, s32[3,1,16]{2,1,0:T(1,128)} %bitcast.1), custom_call_target="tpu_custom_call" | custom-call | tf_op jit(solution)/shard_map/pallas_call | solution.py:409
  54.9 1.2 %shard_map.102 = (bf16[1,48,2048]{2,1,0:T(8,128)(2,1)}, bf16[1,48,2048]{2,1,0:T(8,128)(2,1)}, bf16[1,48,2048]{2,1,0:T(8,128)(2,1)}, bf16[1,48,2048]{2,1,0:T(8,128)(2,1)}, f32[2,128]{1,0:T(2,128)}) custom-call(bf16[4,8,48,256]{3,2,1,0:T(8,128)(2,1)S(1)} %get-tuple-element.12.land, f32[2,128]{1,0:T(2,128)S(1)} %get-tuple-element.13.gain), custom_call_target="tpu_custom_call" | custom-call | tf_op jit(solution)/shard_map/pallas_call | solution.py:453

commit v8 on v6

--- a/solution.py
+++ b/solution.py
@@ -280,24 +280,32 @@
         hg_copies[i, n].start()
 
     gain_k = jnp.zeros((1, HD), F32)
+    gain_q = jnp.zeros((1, HD), F32)
     dks = []
-    for slot in (2, 1, 0):
-        dscore(slot)
+
+    def do_dk(slot, total_k):
         for h, at in both:
             dk = dot(dsc[h, span(slot), :], qs[h]) * LN2
-            gain_k = gain_k + jnp.sum(dk * kunit[h, span(slot), :], axis=0, keepdims=True)
+            total_k = total_k + jnp.sum(dk * kunit[h, span(slot), :], axis=0, keepdims=True)
             if slot > 0:
                 hg_out[0, slot - 1, :, at] = dk.astype(BF16)
             else:
                 dks.append(dk)
         if slot > 0:
             send_near(0, slot - 1)
-    gain_q = jnp.zeros((1, HD), F32)
-    dqs = []
+        return total_k
+
+    dscore(2)
+    gain_k = do_dk(2, gain_k)
+    dscore(1)
+    dscore(0)
     for h, at in both:
         dq = dot(knt[h], dsc[h]).T * SCALE
         gain_q = gain_q + jnp.sum(dq * qunit[h], axis=0, keepdims=True)
-        dqs.append(dq)
+        ob[1, :, at] = norm_backward(qunit[h], qrb[h], g0, dq).astype(BF16)
+    send_out(1)
+    gain_k = do_dk(1, gain_k)
+    gain_k = do_dk(0, gain_k)
 
     stages = (
         (gring, me, ring, ring_id),
@@ -330,9 +338,6 @@
         for h, at in both:
             hg_out[1, n, :, at] = dot(expo[h, span(n + 1), :], doscs[h]).astype(BF16)
         send_near(1, n)
-    for h, at in both:
-        ob[1, :, at] = norm_backward(qunit[h], qrb[h], g0, dqs[h]).astype(BF16)
-    send_out(1)
     hg_copies[0, 0].wait_recv()
     hg_copies[0, 1].wait_recv()
     for h, at in both:

time: 55.9 us -> 59.3 us (1.061)
  Pallas kernels: 55.1 us -> 58.5 us
    pallas_call x1, Pallas kernels: 54.2 us -> 57.6 us  [local(): pl.pallas_call(functools.partial(kernel, sizes), out_shape=landing, in_sp...]
where the time goes in v8:
time: 59.3 us; the launch traced here: 59.2 us
  Pallas kernels  58.5 us (99%)
  between operations  0.64 us (1%)
    pallas_call x1, Pallas kernels, local(): pl.pallas_call(functools.partial(kernel, sizes), out_shape=landing, in_sp...  57.6 us

profile of v8, /device:TPU:1, one launch (start us, length us, event | category | flops | bytes accessed | tf_op | source)
XLA Modules:
  0.0 59.2 jit_solution(175332859621984473)
XLA Ops:
  0.6 57.6 %shard_map.101 = (bf16[4,48,2048]{2,1,0:T(8,128)(2,1)S(1)}, f32[2,128]{1,0:T(2,128)S(1)}) custom-call(bf16[1,48,2048]{2,1,0:T(8,128)(2,1)} %q_in.1, bf16[1,48,2048]{2,1,0:T(8,128)(2,1)} %k_in.1, bf16[1,48,2048]{2,1,0:T(8,128)(2,1)} %v_in.1, bf16[1,48,2048]{2,1,0:T(8,128)(2,1)} %d_in.1, f32[2,128]{1,0:T(2,128)} %gains_in.1, s32[3,1,16]{2,1,0:T(1,128)} %bitcast.1), custom_call_target="tpu_custom_call" | custom-call | tf_op jit(solution)/shard_map/pallas_call | solution.py:408
  58.2 0.9 %shard_map.102 = (bf16[1,48,2048]{2,1,0:T(8,128)(2,1)}, bf16[1,48,2048]{2,1,0:T(8,128)(2,1)}, bf16[1,48,2048]{2,1,0:T(8,128)(2,1)}, bf16[1,48,2048]{2,1,0:T(8,128)(2,1)}, f32[2,128]{1,0:T(2,128)}) custom-call(bf16[4,48,2048]{2,1,0:T(8,128)(2,1)S(1)} %get-tuple-element.12.land, f32[2,128]{1,0:T(2,128)S(1)} %get-tuple-element.13.gain), custom_call_target="tpu_custom_call" | custom-call | tf_op jit(solution)/shard_map/pallas_call | solution.py:452

commit v9 on v6

--- a/solution.py
+++ b/solution.py
@@ -333,21 +333,20 @@
     for h, at in both:
         ob[1, :, at] = norm_backward(qunit[h], qrb[h], g0, dqs[h]).astype(BF16)
     send_out(1)
+    gain_start(1, gain_end(0))
     hg_copies[0, 0].wait_recv()
     hg_copies[0, 1].wait_recv()
     for h, at in both:
         dk = dks[h] + hg_in[0, 0, :, at].astype(F32) + hg_in[0, 1, :, at].astype(F32)
         ob[3, :, at] = norm_backward(kunit[h, span(0), :], krb[h], g1, dk).astype(BF16)
-    gain_start(1, gain_end(0))
     send_out(3)
     hg_copies[1, 0].wait_recv()
     hg_copies[1, 1].wait_recv()
     for h, at in both:
         dv = dot(expo[h, span(0), :], doscs[h])
         ob[2, :, at] = (dv + hg_in[1, 0, :, at].astype(F32) + hg_in[1, 1, :, at].astype(F32)).astype(BF16)
-    send_out(2, 1, heads // 2)
     gain_start(2, gain_end(1))
-    send_out(2, heads // 2, heads)
+    send_out(2)
     gain_out[...] = gain_end(2)[0:2, :] * (1.0 / math.sqrt(total))
 
     def wait_sent(count):

time: 55.9 us -> 57.5 us (1.029)
  Pallas kernels: 55.1 us -> 56.3 us
    pallas_call x1, Pallas kernels: 54.2 us -> 55.4 us  [local(): pl.pallas_call(functools.partial(kernel, sizes), out_shape=landing, in_sp...]
where the time goes in v9:
time: 57.5 us; the launch traced here: 57 us
  Pallas kernels  56.3 us (98%)
  between operations  0.64 us (1%)
    pallas_call x1, Pallas kernels, local(): pl.pallas_call(functools.partial(kernel, sizes), out_shape=landing, in_sp...  55.4 us

profile of v9, /device:TPU:1, one launch (start us, length us, event | category | flops | bytes accessed | tf_op | source)
XLA Modules:
  0.0 57.0 jit_solution(6817961841078826511)
XLA Ops:
  0.6 55.4 %shard_map.101 = (bf16[4,48,2048]{2,1,0:T(8,128)(2,1)S(1)}, f32[2,128]{1,0:T(2,128)S(1)}) custom-call(bf16[1,48,2048]{2,1,0:T(8,128)(2,1)} %q_in.1, bf16[1,48,2048]{2,1,0:T(8,128)(2,1)} %k_in.1, bf16[1,48,2048]{2,1,0:T(8,128)(2,1)} %v_in.1, bf16[1,48,2048]{2,1,0:T(8,128)(2,1)} %d_in.1, f32[2,128]{1,0:T(2,128)} %gains_in.1, s32[3,1,16]{2,1,0:T(1,128)} %bitcast.1), custom_call_target="tpu_custom_call" | custom-call | tf_op jit(solution)/shard_map/pallas_call | solution.py:402
  56.1 0.9 %shard_map.102 = (bf16[1,48,2048]{2,1,0:T(8,128)(2,1)}, bf16[1,48,2048]{2,1,0:T(8,128)(2,1)}, bf16[1,48,2048]{2,1,0:T(8,128)(2,1)}, bf16[1,48,2048]{2,1,0:T(8,128)(2,1)}, f32[2,128]{1,0:T(2,128)}) custom-call(bf16[4,48,2048]{2,1,0:T(8,128)(2,1)S(1)} %get-tuple-element.12.land, f32[2,128]{1,0:T(2,128)S(1)} %get-tuple-element.13.gain), custom_call_target="tpu_custom_call" | custom-call | tf_op jit(solution)/shard_map/pallas_call | solution.py:446

commit v10 on v9

--- a/solution.py
+++ b/solution.py
@@ -333,20 +333,20 @@
     for h, at in both:
         ob[1, :, at] = norm_backward(qunit[h], qrb[h], g0, dqs[h]).astype(BF16)
     send_out(1)
-    gain_start(1, gain_end(0))
     hg_copies[0, 0].wait_recv()
     hg_copies[0, 1].wait_recv()
     for h, at in both:
         dk = dks[h] + hg_in[0, 0, :, at].astype(F32) + hg_in[0, 1, :, at].astype(F32)
         ob[3, :, at] = norm_backward(kunit[h, span(0), :], krb[h], g1, dk).astype(BF16)
     send_out(3)
+    gain_start(1, gain_end(0))
     hg_copies[1, 0].wait_recv()
     hg_copies[1, 1].wait_recv()
     for h, at in both:
         dv = dot(expo[h, span(0), :], doscs[h])
         ob[2, :, at] = (dv + hg_in[1, 0, :, at].astype(F32) + hg_in[1, 1, :, at].astype(F32)).astype(BF16)
+    send_out(2)
     gain_start(2, gain_end(1))
-    send_out(2)
     gain_out[...] = gain_end(2)[0:2, :] * (1.0 / math.sqrt(total))
 
     def wait_sent(count):

time: 57.5 us -> 54.8 us (0.953)
  Pallas kernels: 56.3 us -> 53.8 us
    pallas_call x1, Pallas kernels: 55.4 us -> 52.8 us  [local(): pl.pallas_call(functools.partial(kernel, sizes), out_shape=landing, in_sp...]
where the time goes in v10:
time: 54.8 us; the launch traced here: 54.4 us
  Pallas kernels  53.8 us (98%)
  between operations  0.64 us (1%)
    pallas_call x1, Pallas kernels, local(): pl.pallas_call(functools.partial(kernel, sizes), out_shape=landing, in_sp...  52.8 us

profile of v10, /device:TPU:1, one launch (start us, length us, event | category | flops | bytes accessed | tf_op | source)
XLA Modules:
  0.0 54.4 jit_solution(16120958676392094263)
XLA Ops:
  0.6 52.8 %shard_map.101 = (bf16[4,48,2048]{2,1,0:T(8,128)(2,1)S(1)}, f32[2,128]{1,0:T(2,128)S(1)}) custom-call(bf16[1,48,2048]{2,1,0:T(8,128)(2,1)} %q_in.1, bf16[1,48,2048]{2,1,0:T(8,128)(2,1)} %k_in.1, bf16[1,48,2048]{2,1,0:T(8,128)(2,1)} %v_in.1, bf16[1,48,2048]{2,1,0:T(8,128)(2,1)} %d_in.1, f32[2,128]{1,0:T(2,128)} %gains_in.1, s32[3,1,16]{2,1,0:T(1,128)} %bitcast.1), custom_call_target="tpu_custom_call" | custom-call | tf_op jit(solution)/shard_map/pallas_call | solution.py:402
  53.5 0.9 %shard_map.102 = (bf16[1,48,2048]{2,1,0:T(8,128)(2,1)}, bf16[1,48,2048]{2,1,0:T(8,128)(2,1)}, bf16[1,48,2048]{2,1,0:T(8,128)(2,1)}, bf16[1,48,2048]{2,1,0:T(8,128)(2,1)}, f32[2,128]{1,0:T(2,128)}) custom-call(bf16[4,48,2048]{2,1,0:T(8,128)(2,1)S(1)} %get-tuple-element.12.land, f32[2,128]{1,0:T(2,128)S(1)} %get-tuple-element.13.gain), custom_call_target="tpu_custom_call" | custom-call | tf_op jit(solution)/shard_map/pallas_call | solution.py:446
